TPU v7x, 256 devices: a whole 4x4x8 slice. The times are simulated.
256 devices in a mesh: tm: 8 (over y, core), space: 32 (over z, x).
Axes of the slice: x: 4, y: 4, z: 8, core: 2. Of those that a mesh axis runs over, the one named last changes fastest.
Arguments:
- observed: float32 [16, 192, 1440], P('tm', 'space'), may hold values from -8 to 8
- noise_var: float32 [16], replicated, may hold values from 0.05 to 1
- spectral_var: float32 [1440, 192], P('space'), may hold values from 0.2 to 5
- time_scale: float32 [1440, 192], P('space'), may hold values from 1.5 to 4
Outputs:
- smoothed: float32 [16, 192, 1440], P('tm', 'space')
All inputs are finite; a program needn't handle non-finite values.
Results may differ from a plain program's by a relative error of at most 0.00007.
Values sent between devices are 32-bit elements; how exact they have to be, the bound alone decides.
No kernel may reach another device: no remote copies, remote signals or barrier semaphores. Data moves between devices by JAX's collectives and lax.ppermute only.
A program may use at most 64 MiB of HBM per device.

v0:
```python
import math

import jax
import jax.numpy as jnp
from jax import lax
from jax.sharding import PartitionSpec as P

HIGHEST = lax.Precision.HIGHEST
ROOT_FIVE = 2.23606797749979
NILPOTENT = ((1.0, 1.0, 0.0), (0.0, 1.0, 1.0), (-1.0, -3.0, -2.0))
NILPOTENT_SQUARED = ((1.0, 2.0, 1.0), (-1.0, -2.0, -1.0), (1.0, 2.0, 1.0))
STATIONARY = ((1.0, 0.0, -1.0 / 3.0), (0.0, 1.0 / 3.0, 0.0), (-1.0 / 3.0, 0.0, 1.0))


def lon_basis(size):
    mode_index = lax.broadcasted_iota(jnp.int32, (size, size), 0)
    longitude = lax.broadcasted_iota(jnp.int32, (size, size), 1)
    half_size = size // 2
    sine_rows = mode_index > half_size
    frequency = jnp.where(sine_rows, mode_index - half_size, mode_index)
    radians = (frequency * longitude % size).astype(jnp.float32) * (2.0 * math.pi / size)
    waveform = jnp.where(sine_rows, jnp.sin(radians), jnp.cos(radians))
    edge_rows = (mode_index == 0) | (mode_index == half_size)
    weight = jnp.where(edge_rows, math.sqrt(1.0 / size), math.sqrt(2.0 / size))
    return waveform * weight


def lat_basis(size):
    wavenumber = lax.broadcasted_iota(jnp.int32, (size, size), 0)
    latitude = lax.broadcasted_iota(jnp.int32, (size, size), 1)
    radians = (wavenumber * (2 * latitude + 1) % (4 * size)).astype(jnp.float32) * (
        math.pi / (2.0 * size)
    )
    weight = jnp.where(wavenumber == 0, math.sqrt(1.0 / size), math.sqrt(2.0 / size))
    return jnp.cos(radians) * weight


def mat_mul(left, right):
    return [
        [
            left[across][0] * right[0][within]
            + left[across][1] * right[1][within]
            + left[across][2] * right[2][within]
            for within in range(3)
        ]
        for across in range(3)
    ]


def mat_vec(matrix, vector):
    return [
        matrix[across][0] * vector[0]
        + matrix[across][1] * vector[1]
        + matrix[across][2] * vector[2]
        for across in range(3)
    ]


def transposed(matrix):
    return [[matrix[within][across] for within in range(3)] for across in range(3)]


def inverted(matrix):
    cofactor = [
        [
            matrix[1][1] * matrix[2][2] - matrix[1][2] * matrix[2][1],
            matrix[0][2] * matrix[2][1] - matrix[0][1] * matrix[2][2],
            matrix[0][1] * matrix[1][2] - matrix[0][2] * matrix[1][1],
        ],
        [
            matrix[1][2] * matrix[2][0] - matrix[1][0] * matrix[2][2],
            matrix[0][0] * matrix[2][2] - matrix[0][2] * matrix[2][0],
            matrix[0][2] * matrix[1][0] - matrix[0][0] * matrix[1][2],
        ],
        [
            matrix[1][0] * matrix[2][1] - matrix[1][1] * matrix[2][0],
            matrix[0][1] * matrix[2][0] - matrix[0][0] * matrix[2][1],
            matrix[0][0] * matrix[1][1] - matrix[0][1] * matrix[1][0],
        ],
    ]
    determinant = (
        matrix[0][0] * cofactor[0][0]
        + matrix[0][1] * cofactor[1][0]
        + matrix[0][2] * cofactor[2][0]
    )
    return [[cofactor[across][within] / determinant for within in range(3)] for across in range(3)]


def model_terms(variance, scale):
    decay_rate = ROOT_FIVE / scale
    damping = jnp.exp(-decay_rate)
    transition = [
        [
            damping
            * (
                (1.0 if across == within else 0.0)
                + decay_rate * NILPOTENT[across][within]
                + 0.5 * decay_rate * decay_rate * NILPOTENT_SQUARED[across][within]
            )
            for within in range(3)
        ]
        for across in range(3)
    ]
    stationary = [
        [variance * STATIONARY[across][within] for within in range(3)] for across in range(3)
    ]
    carried = mat_mul(mat_mul(transition, stationary), transposed(transition))
    process_noise = [
        [stationary[across][within] - carried[across][within] for within in range(3)]
        for across in range(3)
    ]
    return (transition, stationary, process_noise)


def predict_cov(covariance, transition, process_noise):
    carried = mat_mul(mat_mul(transition, covariance), transposed(transition))
    return [
        [carried[across][within] + process_noise[across][within] for within in range(3)]
        for across in range(3)
    ]


def gain_and_cov(predicted_cov, noise):
    innovation_var = predicted_cov[0][0] + noise
    kalman_gain = [predicted_cov[across][0] / innovation_var for across in range(3)]
    covariance = [
        [
            predicted_cov[across][within] - kalman_gain[across] * predicted_cov[0][within]
            for within in range(3)
        ]
        for across in range(3)
    ]
    return (kalman_gain, covariance)


def smooth_series(spectra, noise_var, variance, scale):
    transition, stationary, process_noise = model_terms(variance, scale)
    zeros = jnp.zeros_like(variance)

    def forward(carry, inputs):
        mean_state, covariance = carry
        observed, noise = inputs
        predicted_cov = predict_cov(covariance, transition, process_noise)
        smoother_gain = mat_mul(
            mat_mul(covariance, transposed(transition)), inverted(predicted_cov)
        )
        predicted = mat_vec(transition, mean_state)
        kalman_gain, covariance = gain_and_cov(predicted_cov, noise)
        residual = observed - predicted[0]
        mean_state = [predicted[across] + kalman_gain[across] * residual for across in range(3)]
        return ((mean_state, covariance), (mean_state, smoother_gain))

    _, (means, gains) = lax.scan(forward, ([zeros, zeros, zeros], stationary), (spectra, noise_var))

    def backward(later, inputs):
        mean_state, smoother_gain = inputs
        projected = mat_vec(transition, mean_state)
        difference = [later[across] - projected[across] for across in range(3)]
        correction = mat_vec(smoother_gain, difference)
        smoothed_state = [mean_state[across] + correction[across] for across in range(3)]
        return (smoothed_state, smoothed_state[0])

    last_state = [means[across][-1] for across in range(3)]
    earlier_means = [means[across][:-1] for across in range(3)]
    next_gains = [[gains[across][within][1:] for within in range(3)] for across in range(3)]
    _, field = lax.scan(backward, last_state, (earlier_means, next_gains), reverse=True)
    return jnp.concatenate([field, last_state[0][None]], axis=0)


def per_device(observed, noise_var, spectral_var, time_scale):
    hours_dev, lat_dev, lon_size = observed.shape
    band_count = lax.axis_size("space")
    lat_size = lat_dev * band_count
    modes_dev = lon_size // band_count
    lon_table = lon_basis(lon_size)
    lat_table = lat_basis(lat_size).reshape(lat_size, band_count, lat_dev)
    grid_rows = observed.reshape(hours_dev * lat_dev, lon_size)
    spectra = lax.dot_general(lon_table, grid_rows, (((1,), (1,)), ((), ())), precision=HIGHEST)
    by_mode = lax.all_to_all(spectra, "space", split_axis=0, concat_axis=1, tiled=True)
    by_mode = by_mode.reshape(modes_dev, band_count, hours_dev, lat_dev)
    coefficients = jnp.einsum("msha,nsa->hmn", by_mode, lat_table, precision=HIGHEST)
    flat = coefficients.reshape(hours_dev, modes_dev * lat_size)
    hourly = lax.all_to_all(flat, "tm", split_axis=1, concat_axis=0, tiled=True)
    share = flat.shape[1] // lax.axis_size("tm")
    offset = lax.axis_index("tm") * share
    variance = lax.dynamic_slice_in_dim(spectral_var.reshape(-1), offset, share)
    scale = lax.dynamic_slice_in_dim(time_scale.reshape(-1), offset, share)
    series = smooth_series(hourly, noise_var, variance, scale)
    smooth = lax.all_to_all(series, "tm", split_axis=0, concat_axis=1, tiled=True).reshape(
        hours_dev, modes_dev, lat_size
    )
    latitude_grid = jnp.einsum("hmn,nsa->msha", smooth, lat_table, precision=HIGHEST)
    latitude_grid = latitude_grid.reshape(modes_dev, band_count * hours_dev * lat_dev)
    by_band = lax.all_to_all(latitude_grid, "space", split_axis=1, concat_axis=0, tiled=True)
    field = lax.dot_general(by_band, lon_table, (((0,), (0,)), ((), ())), precision=HIGHEST)
    return field.reshape(hours_dev, lat_dev, lon_size)


def solution(mesh):
    placed = (P("tm", "space", None), P(), P("space", None), P("space", None))
    return jax.shard_map(
        per_device, mesh=mesh, in_specs=placed, out_specs=P("tm", "space", None), check_vma=False
    )
```

profile of v0, /device:TPU:1, one launch (start us, length us, event | category | flops | bytes accessed | tf_op | source)
XLA Modules:
  0.0 235.9 jit_solution(3850184011205409712)
XLA Ops:
  0.0 0.9 copy.27
  1.0 54.0 %fusion.93 = f32[32,12,45]{2,1,0:T(8,128)S(1)} fusion(f32[12,1440,1]{1,0,2:T(8,128)S(1)} %reshape.200, f32[32,45]{1,0:T(8,128)S(1)} %fusion.74, s32[32,45]{1,0:T(8,128)S(1)} %get-tuple-element.1149, s32[32,45]{1,0:T(8,128)S(1)} %get-tuple-element.1150, pred[32,45]{1,0:T(8,128)(4,1)S(1)} %fusion.72), kind=kOutput, calls=%fused_computation.223 | convolution fusion | flops 323481600 | bytes 156960 | tf_op jit(solution)/shard_map/dot_general | solution.py:178
  55.1 0.8 reshape.224
  55.9 11.9 %all-to-all-start = ((f32[32,1,540]{2,1,0:T(1,128)}), f32[32,1,540]{2,1,0:T(1,128)S(1)}, u32[]{:S(2)}, u32[]{:S(2)}) async-start(f32[32,1,540]{2,1,0:T(1,128)} %reshape.224), calls=%async_computation | async-start | bytes 163840 | tf_op jit(solution)/shard_map/all_to_all | solution.py:179
  68.1 8.6 %all-to-all-done = f32[32,1,540]{2,1,0:T(1,128)S(1)} async-done(((f32[32,1,540]{2,1,0:T(1,128)}), f32[32,1,540]{2,1,0:T(1,128)S(1)}, u32[]{:S(2)}, u32[]{:S(2)}) %all-to-all-start) | async-done | bytes 69152 | tf_op jit(solution)/shard_map/all_to_all | solution.py:179
  77.2 0.8 reduce.32
  78.3 1.1 convolution_bitcast_fusion.1
  80.3 6.6 %all-to-all-start.1 = ((f32[2,8,1080]{2,0,1:T(2,128)}), f32[2,8,1080]{2,0,1:T(2,128)S(1)}, u32[]{:S(2)}, u32[]{:S(2)}) async-start(f32[2,8,1080]{2,0,1:T(2,128)} %copy.29), calls=%async_computation.1 | async-start | bytes 147456 | tf_op jit(solution)/shard_map/all_to_all | solution.py:183
  87.2 4.6 %all-to-all-done.1 = f32[2,8,1080]{2,0,1:T(2,128)S(1)} async-done(((f32[2,8,1080]{2,0,1:T(2,128)}), f32[2,8,1080]{2,0,1:T(2,128)S(1)}, u32[]{:S(2)}, u32[]{:S(2)}) %all-to-all-start.1) | async-done | bytes 69152 | tf_op jit(solution)/shard_map/all_to_all | solution.py:183
  91.8 62.9 %while.78 = (s32[]{:T(128)}, f32[1080]{0:T(1024)S(1)}, f32[1080]{0:T(1024)S(1)}, f32[1080]{0:T(1024)S(1)}, f32[1080]{0:T(1024)S(1)}, /*index=5*/f32[1080]{0:T(10...) while((s32[]{:T(128)}, f32[1080]{0:T(1024)S(1)}, ...), condition=%wide.region_1.2_spmd.clone, body=%wide.region_0.1_spmd.clone.sunk | while | flops 305643 | bytes 1011360 | solution.py:153
  94.2 0.7 multiply_subtract_fusion.16
  98.1 0.7 multiply_subtract_fusion.16
  102.0 0.7 multiply_subtract_fusion.16
  154.9 7.5 %while.77 = (s32[]{:T(128)}, f32[1080]{0:T(1024)S(1)}, f32[1080]{0:T(1024)S(1)}, f32[1080]{0:T(1024)S(1)}, f32[15,1080]{1,0:T(8,128)S(1)}, /*index=5*/f32[15,108...) while((s32[]{:T(128)}, f32[1080]{0:T(1024)S(1)}, ...), condition=%wide.region_3.4_spmd, body=%wide.region_2.3_spmd.sunk | while | flops 38883 | bytes 272453 | solution.py:166
  162.4 0.7 all_to_all.56
  163.1 4.0 %all-to-all-start.2 = ((f32[8,2,1080]{2,1,0:T(2,128)}), f32[8,2,1080]{2,1,0:T(2,128)S(1)}, u32[]{:S(2)}, u32[]{:S(2)}) async-start(f32[8,2,1080]{2,1,0:T(2,128)} %all_to_all.56), calls=%async_computation.2 | async-start | bytes 147456 | tf_op jit(solution)/shard_map/all_to_all | solution.py:189
  167.2 4.9 %all-to-all-done.2 = f32[8,2,1080]{2,1,0:T(2,128)S(1)} async-done(((f32[8,2,1080]{2,1,0:T(2,128)}), f32[8,2,1080]{2,1,0:T(2,128)S(1)}, u32[]{:S(2)}, u32[]{:S(2)}) %all-to-all-start.2) | async-done | bytes 69152 | tf_op jit(solution)/shard_map/all_to_all | solution.py:189
  172.2 1.1 convolution_bitcast_fusion
  173.5 0.8 reshape.226
  174.3 4.0 %all-to-all-start.3 = ((f32[32,1,540]{2,1,0:T(1,128)}), f32[32,1,540]{2,1,0:T(1,128)S(1)}, u32[]{:S(2)}, u32[]{:S(2)}) async-start(f32[32,1,540]{2,1,0:T(1,128)} %reshape.226), calls=%async_computation.3 | async-start | bytes 163840 | tf_op jit(solution)/shard_map/all_to_all | solution.py:194
  178.4 8.8 %all-to-all-done.3 = f32[32,1,540]{2,1,0:T(1,128)S(1)} async-done(((f32[32,1,540]{2,1,0:T(1,128)}), f32[32,1,540]{2,1,0:T(1,128)S(1)}, u32[]{:S(2)}, u32[]{:S(2)}) %all-to-all-start.3) | async-done | bytes 69152 | tf_op jit(solution)/shard_map/all_to_all | solution.py:194
  187.2 0.8 reduce.33
  188.4 46.8 %fusion.15 = f32[2,6,1440]{2,1,0:T(8,128)S(1)} fusion(f32[2,6,1440]{2,1,0:T(8,128)S(1)} %dot_general.20, f32[1440]{0:T(1024)S(1)} %fusion.79, s32[1440]{0:T(1024)S(1)} %iota_add_fusion, pred[1440]{0:T(1024)(128)(4,1)S(1)} %iota_compare_fusion.2), kind=kOutput, calls=%fused_computation.97 | convolution fusion | flops 323481600 | bytes 151200 | tf_op jit(solution)/shard_map/dot_general | solution.py:195
  235.3 0.7 copy.34
  (760 shorter events, 65.7 us)
Async XLA Ops:
  55.0 12.8 %copy-start = (f32[45,192]{1,0:T(8,128)S(1)}, f32[45,192]{1,0:T(8,128)}, u32[]{:S(2)}) copy-start(f32[45,192]{1,0:T(8,128)} %param.11) | copy-start | bytes 103684
  55.0 12.9 %copy-start.1 = (f32[45,192]{1,0:T(8,128)S(1)}, f32[45,192]{1,0:T(8,128)}, u32[]{:S(2)}) copy-start(f32[45,192]{1,0:T(8,128)} %param.10) | copy-start | bytes 103684
  55.9 20.8 %all-to-all-start = ((f32[32,1,540]{2,1,0:T(1,128)}), f32[32,1,540]{2,1,0:T(1,128)S(1)}, u32[]{:S(2)}, u32[]{:S(2)}) async-start(f32[32,1,540]{2,1,0:T(1,128)} %reshape.224), calls=%async_computation | async-start | bytes 163840 | tf_op jit(solution)/shard_map/all_to_all | solution.py:179
  80.3 11.5 %all-to-all-start.1 = ((f32[2,8,1080]{2,0,1:T(2,128)}), f32[2,8,1080]{2,0,1:T(2,128)S(1)}, u32[]{:S(2)}, u32[]{:S(2)}) async-start(f32[2,8,1080]{2,0,1:T(2,128)} %copy.29), calls=%async_computation.1 | async-start | bytes 147456 | tf_op jit(solution)/shard_map/all_to_all | solution.py:183
  86.8 4.9 %copy-start.2 = (f32[16]{0:T(128)S(1)}, f32[16]{0:T(128)}, u32[]{:S(2)}) copy-start(f32[16]{0:T(128)} %param.9) | copy-start | bytes 196
  163.1 8.9 %all-to-all-start.2 = ((f32[8,2,1080]{2,1,0:T(2,128)}), f32[8,2,1080]{2,1,0:T(2,128)S(1)}, u32[]{:S(2)}, u32[]{:S(2)}) async-start(f32[8,2,1080]{2,1,0:T(2,128)} %all_to_all.56), calls=%async_computation.2 | async-start | bytes 147456 | tf_op jit(solution)/shard_map/all_to_all | solution.py:189
  174.3 12.9 %all-to-all-start.3 = ((f32[32,1,540]{2,1,0:T(1,128)}), f32[32,1,540]{2,1,0:T(1,128)S(1)}, u32[]{:S(2)}, u32[]{:S(2)}) async-start(f32[32,1,540]{2,1,0:T(1,128)} %reshape.226), calls=%async_computation.3 | async-start | bytes 163840 | tf_op jit(solution)/shard_map/all_to_all | solution.py:194
where the time goes:
time: 237 us; the launch traced here: 236 us
  matrix products  103 us (43%)
  local copies, waits for them, and re-layouts  46.9 us (20%)
  waiting for transfers between devices  26.9 us (11%)
  starting transfers between devices  26.5 us (11%)
  other arithmetic  26.4 us (11%)
  loops' own time  5.59 us (2%)
    dot_general x1, matrix products, per_device(): lax.dot_general(lon_table, grid_rows, (((1,), (1,)), ((), ())), precision...  54 us
    dot_general x1, matrix products, per_device(): lax.dot_general(by_band, lon_table, (((0,), (0,)), ((), ())), precision=H...  46.8 us
    dynamic_update_slice x192, local copies, waits for them, and re-layouts, smooth_series(): lax.scan(forward, ([zeros, zeros, zeros], stationary), (spectra, noise_var))  23.7 us
    all_to_all x1, starting transfers between devices, per_device(): lax.all_to_all(spectra, 'space', split_axis=0, concat_axis=1, tiled=True)  11.9 us
    sub x16, other arithmetic, gain_and_cov(): predicted_cov[across][within]  10.8 us
    add x16, other arithmetic, forward(): predicted[across] + kalman_gain[across] * residual  10.5 us
    dynamic_slice x32, local copies, waits for them, and re-layouts, smooth_series(): lax.scan(forward, ([zeros, zeros, zeros], stationary), (spectra, noise_var))  9.88 us
    all_to_all x1, waiting for transfers between devices, per_device(): lax.all_to_all(latitude_grid, 'space', split_axis=1, concat_axis=0, tiled...  8.79 us
  transfers between devices with their start and end apart: 4, of which 4 were waited for; matrix products, arithmetic and copies ran while one was open for 0% of the time, Pallas kernels for 0%

commit v1 on v0

v1 whole, which is shorter than its diff:
```python
import functools
import math

import jax
import jax.numpy as jnp
import ml_dtypes
import numpy as np
from jax import lax
from jax.experimental import pallas as pl
from jax.experimental.pallas import tpu as pltpu
from jax.sharding import PartitionSpec as P

ROOT_FIVE = 2.23606797749979
NILPOTENT = ((1.0, 1.0, 0.0), (0.0, 1.0, 1.0), (-1.0, -3.0, -2.0))
NILPOTENT_SQUARED = ((1.0, 2.0, 1.0), (-1.0, -2.0, -1.0), (1.0, 2.0, 1.0))
STATIONARY = ((1.0, 0.0, -1.0 / 3.0), (0.0, 1.0 / 3.0, 0.0), (-1.0 / 3.0, 0.0, 1.0))
F32 = jnp.float32
BF16 = jnp.bfloat16
SUB = 8
LANES = 128
MIB = 2**20


def two_halves(table):
    high = table.astype(ml_dtypes.bfloat16)
    low = (table - high.astype(np.float64)).astype(ml_dtypes.bfloat16)
    return np.stack([high, low], axis=-3)


def lon_basis(size):
    mode = np.arange(size)[:, None]
    longitude = np.arange(size)[None, :]
    half = size // 2
    sine = mode > half
    frequency = np.where(sine, mode - half, mode)
    radians = (frequency * longitude % size) * (2.0 * math.pi / size)
    weight = np.where((mode == 0) | (mode == half), math.sqrt(1.0 / size), math.sqrt(2.0 / size))
    return np.where(sine, np.sin(radians), np.cos(radians)) * weight


def lat_basis(size):
    wavenumber = np.arange(size)[:, None]
    latitude = np.arange(size)[None, :]
    radians = (wavenumber * (2 * latitude + 1) % (4 * size)) * (math.pi / (2.0 * size))
    weight = np.where(wavenumber == 0, math.sqrt(1.0 / size), math.sqrt(2.0 / size))
    return np.cos(radians) * weight


def lon_tables(size, hour_blocks, bands):
    per_band = size // bands
    slots = -(-per_band // hour_blocks)
    half_slots = slots // 2
    basis = lon_basis(size)
    parity = np.arange(2)[:, None, None, None]
    slot = np.arange(half_slots)[None, :, None, None]
    block = np.arange(hour_blocks)[None, None, :, None]
    band = np.arange(bands)[None, None, None, :]
    within = slots * block + 2 * slot + (band * per_band + parity) % 2
    mode = np.where(within < per_band, per_band * band + within, 0)
    rows = basis[mode] * (within < per_band)[..., None]
    return rows.reshape(2, half_slots, hour_blocks * bands, size)[..., : size // 2]


def split(value):
    high = value.astype(BF16)
    return high, (value - high.astype(F32)).astype(BF16)


def product(value, table_high, table_low):
    rows = value.shape[0]
    high, low = split(value)
    both = jnp.dot(jnp.concatenate([high, low], axis=0), table_high, preferred_element_type=F32)
    return both[:rows] + both[rows:] + jnp.dot(high, table_low, preferred_element_type=F32)


def analyse_kernel(x_ref, table_ref, out_ref, folded, slots_of, table, sems):
    hours, lats, lon = x_ref.shape
    half_slots = table_ref.shape[1]
    copies = [
        pltpu.make_async_copy(table_ref.at[p, k], table.at[p, k], sems.at[p, k])
        for p in range(2)
        for k in range(half_slots)
    ]
    for copy in copies:
        copy.start()
    folded[...] = jnp.zeros_like(folded)
    slots_of[...] = jnp.zeros_like(slots_of)
    for h in range(hours):
        left = x_ref[h, :, : lon // 2]
        right = x_ref[h, :, lon // 2 :]
        folded[0, h * SUB : h * SUB + lats, :] = left + right
        folded[1, h * SUB : h * SUB + lats, :] = left - right
    rows = hours * SUB
    for p in range(2):
        value = folded[p]
        for k in range(half_slots):
            at = p * half_slots + k
            copies[at].wait()
            slots_of[at * rows : (at + 1) * rows, :] = product(value, table[p, k, 0], table[p, k, 1])
    out_ref[...] = slots_of[...].T


def gains_kernel(half_slots, where_ref, noise_ref, var_ref, scale_ref, trans_ref, gain_ref, var, scale):
    block = where_ref[0]
    odd = where_ref[1]
    last = var_ref.shape[0] - 1
    var[...] = jnp.ones_like(var)
    scale[...] = jnp.ones_like(scale)
    for p in range(2):
        for k in range(half_slots):
            row = jnp.minimum(2 * half_slots * block + 2 * k + (odd + p) % 2, last)
            at = p * half_slots + k
            var[at : at + 1, :] = var_ref[pl.ds(row, 1), :]
            scale[at : at + 1, :] = scale_ref[pl.ds(row, 1), :]
    variance = var[...]
    rate = ROOT_FIVE / scale[...]
    damping = jnp.exp(-rate)
    a = [
        [
            damping
            * (
                (1.0 if i == j else 0.0)
                + rate * NILPOTENT[i][j]
                + 0.5 * rate * rate * NILPOTENT_SQUARED[i][j]
            )
            for j in range(3)
        ]
        for i in range(3)
    ]
    for i in range(3):
        for j in range(3):
            trans_ref[3 * i + j] = a[i][j]

    def carried(cov):
        ap = [[a[i][0] * cov[0][j] + a[i][1] * cov[1][j] + a[i][2] * cov[2][j] for j in range(3)] for i in range(3)]
        upper = {
            (i, j): ap[i][0] * a[j][0] + ap[i][1] * a[j][1] + ap[i][2] * a[j][2]
            for i in range(3)
            for j in range(i, 3)
        }
        return [[upper[min(i, j), max(i, j)] for j in range(3)] for i in range(3)]

    cov = [[variance * STATIONARY[i][j] for j in range(3)] for i in range(3)]
    start = carried(cov)
    noise_cov = [[cov[i][j] - start[i][j] for j in range(3)] for i in range(3)]
    for h in range(gain_ref.shape[0]):
        noise = noise_ref[h]
        moved = carried(cov)
        pm = {(i, j): moved[i][j] + noise_cov[i][j] for i in range(3) for j in range(i, 3)}
        inverse = 1.0 / (pm[0, 0] + noise)
        k = [pm[0, j] * inverse for j in range(3)]
        for j in range(3):
            gain_ref[h, j] = k[j]
        gain_ref[h, 3] = inverse
        first = [noise * k[j] for j in range(3)]
        c11 = pm[1, 1] - k[1] * pm[0, 1]
        c12 = pm[1, 2] - k[1] * pm[0, 2]
        c22 = pm[2, 2] - k[2] * pm[0, 2]
        cov = [[first[0], first[1], first[2]], [first[1], c11, c12], [first[2], c12, c22]]


def smooth_kernel(lats, noise_ref, x_ref, trans_ref, gain_ref, into_ref, back_ref, out_ref, turned, grid, series):
    owners, lanes = x_ref.shape
    hours = gain_ref.shape[0]
    bands = grid.shape[1] // lats
    blocks = owners // bands
    per_block = hours // blocks
    stride = per_block * SUB
    parts, _, width = turned.shape
    for part in range(parts):
        turned[part] = x_ref[part * width : (part + 1) * width, :].T
    per_part = width // bands
    for h in range(per_block):
        for lat in range(lats):
            for part in range(parts):
                rows = turned[part, pl.ds(h * SUB + lat, SUB, stride=stride), :]
                for t in range(per_part):
                    at = ((part * per_part + t) * per_block + h) * SUB
                    grid[at : at + SUB, lat * bands : (lat + 1) * bands] = rows[:, t * bands : (t + 1) * bands]
    series[...] = product(grid[...], into_ref[0], into_ref[1])

    a = [[trans_ref[3 * i + j] for j in range(3)] for i in range(3)]
    scaled = []
    mean = None
    for h in range(hours):
        seen = series[h * SUB : (h + 1) * SUB, :]
        if mean is None:
            error = seen
            mean = [gain_ref[h, j] * error for j in range(3)]
        else:
            ahead = [a[i][0] * mean[0] + a[i][1] * mean[1] + a[i][2] * mean[2] for i in range(3)]
            error = seen - ahead[0]
            mean = [ahead[j] + gain_ref[h, j] * error for j in range(3)]
        scaled.append(error * gain_ref[h, 3])
    adjoint = None
    for h in reversed(range(hours)):
        drop = scaled[h]
        if adjoint is not None:
            drop = drop + (gain_ref[h, 0] * adjoint[0] + gain_ref[h, 1] * adjoint[1] + gain_ref[h, 2] * adjoint[2])
        here = slice(h * SUB, (h + 1) * SUB)
        series[here, :] = series[here, :] - noise_ref[h] * drop
        if adjoint is None:
            adjoint = [-(a[0][j] * drop) for j in range(3)]
        else:
            less = adjoint[0] - drop
            adjoint = [a[0][j] * less + a[1][j] * adjoint[1] + a[2][j] * adjoint[2] for j in range(3)]

    grid[...] = product(series[...], back_ref[0], back_ref[1])
    turned[...] = jnp.zeros_like(turned)
    for h in range(per_block):
        for lat in range(lats):
            for part in range(parts):
                rows = jnp.concatenate(
                    [
                        grid[(t * per_block + h) * SUB : (t * per_block + h + 1) * SUB, lat * bands : (lat + 1) * bands]
                        for t in range(part * per_part, (part + 1) * per_part)
                    ],
                    axis=1,
                )
                turned[part, pl.ds(h * SUB + lat, SUB, stride=stride), :] = rows
    for part in range(parts):
        out_ref[part * width : (part + 1) * width, :] = turned[part].T


def synthesise_kernel(x_ref, table_ref, out_ref, turned):
    hours, lats, lon = out_ref.shape
    half_slots = table_ref.shape[1]
    rows = hours * SUB
    turned[...] = x_ref[...].T
    halves = []
    for p in range(2):
        total = None
        for k in range(half_slots):
            at = p * half_slots + k
            part = product(turned[at * rows : (at + 1) * rows, :], table_ref[p, k, 0], table_ref[p, k, 1])
            total = part if total is None else total + part
        halves.append(total)
    even, odd = halves
    for h in range(hours):
        here = slice(h * SUB, h * SUB + lats)
        out_ref[h, :, : lon // 2] = even[here] + odd[here]
        out_ref[h, :, lon // 2 :] = even[here] - odd[here]


def params(mib):
    return pltpu.CompilerParams(vmem_limit_bytes=mib * MIB)


def per_device(tables, observed, noise_var, spectral_var, time_scale):
    lon_into, lon_back, lat_into, lat_back = tables
    hours_dev, lat_dev, lon_size = observed.shape
    hours = noise_var.shape[0]
    owners = lon_into.shape[-1]
    half_slots = lon_into.shape[1]
    lat_size = lat_into.shape[-1]
    lanes = SUB * hours_dev * SUB
    vmem = pl.BlockSpec(memory_space=pltpu.VMEM)
    smem = pl.BlockSpec(memory_space=pltpu.SMEM)

    sent = pl.pallas_call(
        analyse_kernel,
        out_shape=jax.ShapeDtypeStruct((owners, lanes), F32),
        in_specs=[vmem, pl.BlockSpec(memory_space=pl.ANY)],
        out_specs=vmem,
        scratch_shapes=[
            pltpu.VMEM((2, hours_dev * SUB, lon_size // 2), F32),
            pltpu.VMEM((lanes, owners), F32),
            pltpu.VMEM(lon_into.shape, BF16),
            pltpu.SemaphoreType.DMA((2, half_slots)),
        ],
        compiler_params=params(16),
        name="analyse",
    )(observed, lon_into)
    got = lax.all_to_all(sent, ("tm", "space"), split_axis=0, concat_axis=0, tiled=True)

    where = jnp.stack([lax.axis_index("tm"), lax.axis_index("space") * spectral_var.shape[0] % 2]).astype(jnp.int32)
    transition, gains = pl.pallas_call(
        functools.partial(gains_kernel, half_slots),
        out_shape=(
            jax.ShapeDtypeStruct((9, SUB, lat_size), F32),
            jax.ShapeDtypeStruct((hours, 4, SUB, lat_size), F32),
        ),
        in_specs=[smem, smem, vmem, vmem],
        out_specs=(vmem, vmem),
        scratch_shapes=[pltpu.VMEM((SUB, lat_size), F32)] * 2,
        cost_estimate=pl.CostEstimate(flops=200 * hours * SUB * 256, bytes_accessed=2 * MIB, transcendentals=0),
        name="gains",
    )(where, noise_var, spectral_var, time_scale)

    smooth = pl.pallas_call(
        functools.partial(smooth_kernel, lat_dev),
        out_shape=jax.ShapeDtypeStruct((owners, lanes), F32),
        in_specs=[smem] + [vmem] * 5,
        out_specs=vmem,
        scratch_shapes=[
            pltpu.VMEM((owners // LANES, lanes, LANES), F32),
            pltpu.VMEM((hours * SUB, lat_size), F32),
            pltpu.VMEM((hours * SUB, lat_size), F32),
        ],
        compiler_params=params(16),
        name="smooth",
    )(noise_var, got, transition, gains, lat_into, lat_back)
    back = lax.all_to_all(smooth, ("tm", "space"), split_axis=0, concat_axis=0, tiled=True)

    return pl.pallas_call(
        synthesise_kernel,
        out_shape=jax.ShapeDtypeStruct(observed.shape, F32),
        in_specs=[vmem, vmem],
        out_specs=vmem,
        scratch_shapes=[pltpu.VMEM((lanes, owners), F32)],
        compiler_params=params(16),
        name="synthesise",
    )(back, lon_back)


def solution(mesh):
    placed = (P("tm", "space", None), P(), P("space", None), P("space", None))
    blocks, bands = mesh.shape["tm"], mesh.shape["space"]

    def whole(observed, noise_var, spectral_var, time_scale):
        lon_size = observed.shape[2]
        lat_size = spectral_var.shape[1]
        rows = lon_tables(lon_size, blocks, bands)
        by_lat = lat_basis(lat_size).reshape(lat_size, bands, lat_size // bands)
        by_lat = by_lat.transpose(0, 2, 1).reshape(lat_size, lat_size)
        tables = (
            two_halves(rows.transpose(0, 1, 3, 2)),
            two_halves(rows),
            two_halves(by_lat.T),
            two_halves(by_lat),
        )
        tables = tuple(jnp.asarray(table) for table in tables)
        return jax.shard_map(
            functools.partial(per_device, tables),
            mesh=mesh,
            in_specs=placed,
            out_specs=P("tm", "space", None),
            check_vma=False,
        )(observed, noise_var, spectral_var, time_scale)

    return whole
```

time: 237 us -> 62.2 us (0.26)
  matrix products: 103 us -> 0 us
  local copies, waits for them, and re-layouts: 46.9 us -> 8.15 us
  other arithmetic: 26.4 us -> 0.61 us
  blocking collectives: 0 us -> 18.2 us
  waiting for transfers between devices: 26.9 us -> 9.93 us
  starting transfers between devices: 26.5 us -> 15.7 us
  Pallas kernels: 0 us -> 9.16 us
  loops' own time: 5.59 us -> 0 us
    dot_general x4 -> x0, matrix products: 103 us -> none  [the longest x1 54 us: per_device(): lax.dot_general(lon_table, grid_rows, (((1,), (1,)), ((), ())), precision...]
    dynamic_update_slice x207 -> x0, local copies, waits for them, and re-layouts: 25.6 us -> none  [the longest x192 23.7 us: smooth_series(): lax.scan(forward, ([zeros, zeros, zeros], stationary), (spectra, noise_var))]
    all_to_all x0 -> x1, blocking collectives: none -> 18.2 us  [per_device(): lax.all_to_all(smooth, ('tm', 'space'), split_axis=0, concat_axis=0, tile...]
    all_to_all x4 -> x1, waiting for transfers between devices: 26.9 us -> 9.93 us  [per_device(): lax.all_to_all(sent, ('tm', 'space'), split_axis=0, concat_axis=0, tiled=...]
    add x127 -> x0, other arithmetic: 13.7 us -> none  [the longest x16 10.5 us: forward(): predicted[across] + kalman_gain[across] * residual]
    dynamic_slice x122 -> x0, local copies, waits for them, and re-layouts: 13.5 us -> none  [the longest x32 9.88 us: smooth_series(): lax.scan(forward, ([zeros, zeros, zeros], stationary), (spectra, noise_var))]
    sub x19 -> x0, other arithmetic: 11 us -> none  [the longest x16 10.8 us: gain_and_cov(): predicted_cov[across][within]]
    all_to_all x4 -> x1, starting transfers between devices: 26.5 us -> 15.7 us  [per_device(): lax.all_to_all(sent, ('tm', 'space'), split_axis=0, concat_axis=0, tiled=...]
  transfers between devices with their start and end apart: 4 -> 1, of which waited for: 4 -> 1; matrix products, arithmetic and copies ran while one was open for 0% -> 1% of each run, Pallas kernels for 0% -> 3%
where the time goes in v1:
time: 62.2 us; the launch traced here: 61.8 us
  blocking collectives  18.2 us (29%)
  starting transfers between devices  15.7 us (25%)
  waiting for transfers between devices  9.93 us (16%)
  Pallas kernels  9.16 us (15%)
  local copies, waits for them, and re-layouts  8.15 us (13%)
    all_to_all x1, blocking collectives, per_device(): lax.all_to_all(smooth, ('tm', 'space'), split_axis=0, concat_axis=0, tile...  18.2 us
    all_to_all x1, starting transfers between devices, per_device(): lax.all_to_all(sent, ('tm', 'space'), split_axis=0, concat_axis=0, tiled=...  15.7 us
    all_to_all x1, waiting for transfers between devices, per_device(): lax.all_to_all(sent, ('tm', 'space'), split_axis=0, concat_axis=0, tiled=...  9.93 us
    unnamed x15, local copies, waits for them, and re-layouts  7.43 us
    pallas_call x1, Pallas kernels, per_device(): pl.pallas_call(analyse_kernel, out_shape=jax.ShapeDtypeStruct((owners, la...  4.58 us
    pallas_call x1, Pallas kernels, per_device(): pl.pallas_call(functools.partial(gains_kernel, half_slots), out_shape=(ja...  2.09 us
    pallas_call x1, Pallas kernels, per_device(): pl.pallas_call(functools.partial(smooth_kernel, lat_dev), out_shape=jax.S...  1.67 us
  transfers between devices with their start and end apart: 1, of which 1 were waited for; matrix products, arithmetic and copies ran while one was open for 1% of the time, Pallas kernels for 3%

profile of v1, /device:TPU:1, one launch (start us, length us, event | category | flops | bytes accessed | tf_op | source)
XLA Modules:
  0.0 61.8 jit_solution(10700860807793358480)
XLA Ops:
  0.0 0.0 copy-start.6
  0.0 0.9 %copy.11.x_ref = f32[2,6,1440]{2,1,0:T(8,128)S(1)} copy(f32[2,6,1440]{2,0,1:T(2,128)} %param.8) | data formatting | bytes 138240 | tf_op args[0]
  0.9 0.0 copy-start.1
  0.9 2.2 %copy-done.1 = bf16[2,3,2,720,256]{4,3,2,1,0:T(8,128)(2,1)S(1)} copy-done((bf16[2,3,2,720,256]{4,3,2,1,0:T(8,128)(2,1)S(1)}, bf16[2,3,2,720,256]{4,3,2,1,0:T(8,128)(2,1)}, u32[]{:S(2)}) %copy-start.1) | copy-done | bytes 4423704
  3.2 0.0 copy-start.3
  3.2 0.0 copy-start.4
  3.2 4.6 %analyse.1 = f32[256,128]{1,0:T(8,128)} custom-call(f32[2,6,1440]{2,1,0:T(8,128)S(1)} %copy.11.x_ref, bf16[2,3,2,720,256]{4,3,2,1,0:T(8,128)(2,1)S(1)} %copy-done.1), custom_call_target="tpu_custom_call" | custom-call | tf_op jit(solution)/shard_map/analyse/pallas_call | solution.py:260
  7.8 15.7 %all-to-all-start = ((f32[256,1,128]{2,1,0:T(1,128)}), f32[256,1,128]{2,1,0:T(1,128)S(1)}, u32[]{:S(2)}, u32[]{:S(2)}) async-start(f32[256,1,128]{2,1,0:T(1,128)} %bitcast.1), calls=%async_computation | async-start | bytes 262144 | tf_op jit(solution)/shard_map/all_to_all | solution.py:274
  23.5 0.6 pad_add_fusion.where_ref
  24.1 2.1 %gains.1 = (f32[9,8,192]{2,1,0:T(8,128)}, f32[16,4,8,192]{3,2,1,0:T(8,128)}) custom-call(s32[2]{0:T(128)} %pad_add_fusion.where_ref, f32[16]{0:T(128)} %noise_ref.3, f32[45,192]{1,0:T(8,128)} %var_ref.1, f32[45,192]{1,0:T(8,128)} %scale_ref.1), custom_call_target="tpu_custom_call" | custom-call | flops 6553600 | bytes 2097152 | tf_op jit(solution)/shard_map/gains/pallas_call | solution.py:277
  26.2 9.9 %all-to-all-done = f32[256,1,128]{2,1,0:T(1,128)S(1)} async-done(((f32[256,1,128]{2,1,0:T(1,128)}), f32[256,1,128]{2,1,0:T(1,128)S(1)}, u32[]{:S(2)}, u32[]{:S(2)}) %all-to-all-start) | async-done | bytes 131104 | tf_op jit(solution)/shard_map/all_to_all | solution.py:274
  36.1 0.0 copy-done.6
  36.1 0.0 copy-done.3
  36.1 0.0 copy-done.4
  36.1 0.0 copy-start.2
  36.1 1.0 %copy-done.2 = f32[16,4,8,192]{3,2,1,0:T(8,128)S(1)} copy-done((f32[16,4,8,192]{3,2,1,0:T(8,128)S(1)}, f32[16,4,8,192]{3,2,1,0:T(8,128)}, u32[]{:S(2)}) %copy-start.2) | copy-done | bytes 393240
  37.1 0.0 copy-start.5
  37.1 0.9 %copy-done.5 = f32[9,8,192]{2,1,0:T(8,128)S(1)} copy-done((f32[9,8,192]{2,1,0:T(8,128)S(1)}, f32[9,8,192]{2,1,0:T(8,128)}, u32[]{:S(2)}) %copy-start.5) | copy-done | bytes 55320
  38.0 1.7 %smooth.1 = f32[256,128]{1,0:T(8,128)S(1)} custom-call(f32[16]{0:T(128)S(1)} %copy-done.6, f32[256,128]{1,0:T(8,128)S(1)} %bitcast.10, f32[9,8,192]{2,1,0:T(8,128)S(1)} %copy-done.5, f32[16,4,8,192]{3,2,1,0:T(8,128)S(1)} %copy-done.2, bf16[2,192,192]{2,1,0:T(8,128)(2,1)S(1)} %copy-done.4, bf16[2,192,192]{2,1,0:T(8,128)(2,1)S(1)} %copy-done.3), custom_call_target="tpu_custom_call" | custom-call | tf_op jit(solution)/shard_map/smooth/pallas_call | solution.py:290
  39.7 18.2 %all_to_all.22 = f32[256,1,128]{2,1,0:T(1,128)S(1)} all-to-all(f32[256,1,128]{2,1,0:T(1,128)S(1)} %bitcast.11), channel_id=1, replica_groups=mesh['tm'=8,'space'=32] {'tm','space'}, dimensions={0} | all-to-all | bytes 262144 | tf_op jit(solution)/shard_map/all_to_all | solution.py:303
  57.9 0.0 copy-start
  57.9 2.3 %copy-done = bf16[2,3,2,256,720]{4,3,2,1,0:T(8,128)(2,1)S(1)} copy-done((bf16[2,3,2,256,720]{4,3,2,1,0:T(8,128)(2,1)S(1)}, bf16[2,3,2,256,720]{4,3,2,1,0:T(8,128)(2,1)}, u32[]{:S(2)}) %copy-start) | copy-done | bytes 4423704
  60.3 0.8 %synthesise.1 = f32[2,6,1440]{2,1,0:T(8,128)S(1)} custom-call(f32[256,128]{1,0:T(8,128)S(1)} %bitcast.12, bf16[2,3,2,256,720]{4,3,2,1,0:T(8,128)(2,1)S(1)} %copy-done), custom_call_target="tpu_custom_call" | custom-call | tf_op jit(solution)/shard_map/synthesise/pallas_call | solution.py:305
  61.1 0.7 %copy.14 = f32[2,6,1440]{2,0,1:T(2,128)} copy(f32[2,6,1440]{2,1,0:T(8,128)S(1)} %synthesise.1) | data formatting | bytes 138240 | tf_op jit(solution)/shard_map/synthesise/pallas_call | solution.py:305
Async XLA Ops:
  0.0 36.1 %copy-start.6 = (f32[16]{0:T(128)S(1)}, f32[16]{0:T(128)}, u32[]{:S(2)}) copy-start(f32[16]{0:T(128)} %noise_ref.3) | copy-start | bytes 196
  0.9 2.3 %copy-start.1 = (bf16[2,3,2,720,256]{4,3,2,1,0:T(8,128)(2,1)S(1)}, bf16[2,3,2,720,256]{4,3,2,1,0:T(8,128)(2,1)}, u32[]{:S(2)}) copy-start(bf16[2,3,2,720,256]{4,3,2,1,0:T(8,128)(2,1)} %constant.32.clone.table_ref) | copy-start | bytes 13271044
  3.2 32.9 %copy-start.3 = (bf16[2,192,192]{2,1,0:T(8,128)(2,1)S(1)}, bf16[2,192,192]{2,1,0:T(8,128)(2,1)}, u32[]{:S(2)}) copy-start(bf16[2,192,192]{2,1,0:T(8,128)(2,1)} %constant.34.clone.back_ref) | copy-start | bytes 442372
  3.2 32.9 %copy-start.4 = (bf16[2,192,192]{2,1,0:T(8,128)(2,1)S(1)}, bf16[2,192,192]{2,1,0:T(8,128)(2,1)}, u32[]{:S(2)}) copy-start(bf16[2,192,192]{2,1,0:T(8,128)(2,1)} %constant.33.clone.into_ref) | copy-start | bytes 442372
  7.8 28.3 %all-to-all-start = ((f32[256,1,128]{2,1,0:T(1,128)}), f32[256,1,128]{2,1,0:T(1,128)S(1)}, u32[]{:S(2)}, u32[]{:S(2)}) async-start(f32[256,1,128]{2,1,0:T(1,128)} %bitcast.1), calls=%async_computation | async-start | bytes 262144 | tf_op jit(solution)/shard_map/all_to_all | solution.py:274
  36.1 1.0 %copy-start.2 = (f32[16,4,8,192]{3,2,1,0:T(8,128)S(1)}, f32[16,4,8,192]{3,2,1,0:T(8,128)}, u32[]{:S(2)}) copy-start(f32[16,4,8,192]{3,2,1,0:T(8,128)} %get-tuple-element.8.gain_ref) | copy-start | bytes 1179652
  37.1 0.9 %copy-start.5 = (f32[9,8,192]{2,1,0:T(8,128)S(1)}, f32[9,8,192]{2,1,0:T(8,128)}, u32[]{:S(2)}) copy-start(f32[9,8,192]{2,1,0:T(8,128)} %get-tuple-element.7.trans_ref) | copy-start | bytes 165892
  57.9 2.3 %copy-start = (bf16[2,3,2,256,720]{4,3,2,1,0:T(8,128)(2,1)S(1)}, bf16[2,3,2,256,720]{4,3,2,1,0:T(8,128)(2,1)}, u32[]{:S(2)}) copy-start(bf16[2,3,2,256,720]{4,3,2,1,0:T(8,128)(2,1)} %constant.35.clone.table_ref) | copy-start | bytes 13271044

commit v2 on v1

v2 whole, which is shorter than its diff:
```python
import functools
import math

import jax
import jax.numpy as jnp
import ml_dtypes
import numpy as np
from jax import lax
from jax.experimental import pallas as pl
from jax.experimental.pallas import tpu as pltpu
from jax.sharding import PartitionSpec as P

ROOT_FIVE = 2.23606797749979
NILPOTENT = ((1.0, 1.0, 0.0), (0.0, 1.0, 1.0), (-1.0, -3.0, -2.0))
NILPOTENT_SQUARED = ((1.0, 2.0, 1.0), (-1.0, -2.0, -1.0), (1.0, 2.0, 1.0))
STATIONARY = ((1.0, 0.0, -1.0 / 3.0), (0.0, 1.0 / 3.0, 0.0), (-1.0 / 3.0, 0.0, 1.0))
F32 = jnp.float32
BF16 = jnp.bfloat16
SUB = 8
LANES = 128
STEP = 120
MIB = 2**20


def two_halves(table):
    high = table.astype(ml_dtypes.bfloat16)
    low = (table - high.astype(np.float64)).astype(ml_dtypes.bfloat16)
    return np.stack([high, low], axis=-3)


def lon_basis(size):
    mode = np.arange(size)[:, None]
    longitude = np.arange(size)[None, :]
    half = size // 2
    sine = mode > half
    frequency = np.where(sine, mode - half, mode)
    radians = (frequency * longitude % size) * (2.0 * math.pi / size)
    weight = np.where((mode == 0) | (mode == half), math.sqrt(1.0 / size), math.sqrt(2.0 / size))
    return np.where(sine, np.sin(radians), np.cos(radians)) * weight


def lat_basis(size):
    wavenumber = np.arange(size)[:, None]
    latitude = np.arange(size)[None, :]
    radians = (wavenumber * (2 * latitude + 1) % (4 * size)) * (math.pi / (2.0 * size))
    weight = np.where(wavenumber == 0, math.sqrt(1.0 / size), math.sqrt(2.0 / size))
    return np.cos(radians) * weight


def lon_tables(size, hour_blocks, bands):
    per_band = size // bands
    slots = -(-per_band // hour_blocks)
    half = size // 2
    slot = np.arange(slots)[:, None, None]
    block = np.arange(hour_blocks)[None, :, None]
    band = np.arange(bands)[None, None, :]
    within = slots * block + slot + 0 * band
    used = within < per_band
    mode = np.where(used, per_band * band + within, 0)
    rows = (lon_basis(size)[mode] * used[..., None]).reshape(slots, hour_blocks * bands, size)
    sine = mode > half
    frequency = np.where(sine, mode - half, mode)
    ahead = np.arange(size // STEP)[:, None, None, None] * STEP
    radians = (frequency * ahead % size) * (2.0 * math.pi / size)
    straight = np.where(used, np.cos(radians), 0.0)
    crossed = np.where(used & (mode % half != 0), np.sin(radians), 0.0) * np.where(sine, 1.0, -1.0)
    crossed = np.roll(crossed, bands // 2, axis=-1)
    turns = np.stack([straight, crossed]).reshape(2, size // STEP, slots, hour_blocks * bands)
    head = np.zeros((slots, hour_blocks * bands, LANES))
    head[..., :STEP] = rows[..., :STEP]
    return head, turns.transpose(2, 0, 1, 3).astype(np.float32)


def split(value):
    high = value.astype(BF16)
    return high, (value - high.astype(F32)).astype(BF16)


def product(value, table_high, table_low):
    rows = value.shape[0]
    high, low = split(value)
    both = jnp.dot(jnp.concatenate([high, low], axis=0), table_high, preferred_element_type=F32)
    return both[:rows] + both[rows:] + jnp.dot(high, table_low, preferred_element_type=F32)


def partners(value, bands):
    half = bands // 2
    width = value.shape[1]
    upper = lax.broadcasted_iota(jnp.int32, value.shape, 1) % bands >= half
    return jnp.where(upper, pltpu.roll(value, half, 1), pltpu.roll(value, width - half, 1))


def analyse_kernel(bands, x_hbm, table_hbm, turns_hbm, out_ref, x, table, turns, flat, blocks, slots_of, sems):
    lats, hours, lon = x.shape
    slots = table.shape[0]
    steps = lon // STEP
    rows = 2 * SUB
    fetch = [pltpu.make_async_copy(x_hbm, x, sems.at[0]), pltpu.make_async_copy(turns_hbm, turns, sems.at[1])]
    fetch += [pltpu.make_async_copy(table_hbm.at[m], table.at[m], sems.at[2 + m]) for m in range(slots)]
    fetch[0].start()
    fetch[2].start()
    fetch[1].start()
    for m in range(1, slots):
        fetch[2 + m].start()
    flat[...] = jnp.zeros_like(flat)
    blocks[...] = jnp.zeros_like(blocks)
    slots_of[...] = jnp.zeros_like(slots_of)
    fetch[0].wait()
    for lat in range(lats):
        flat[lat * hours : (lat + 1) * hours, :] = x[lat]
    for b in range(steps):
        blocks[b * rows : (b + 1) * rows, :STEP] = flat[:, b * STEP : (b + 1) * STEP]
    value = blocks[...]
    for m in range(slots):
        fetch[2 + m].wait()
        part = product(value, table[m, 0], table[m, 1])
        if m == 0:
            fetch[1].wait()
        straight = crossed = None
        for b in range(steps):
            here = part[b * rows : (b + 1) * rows]
            plain = here * turns[m, 0, b : b + 1, :]
            cross = here * turns[m, 1, b : b + 1, :]
            straight = plain if straight is None else straight + plain
            crossed = cross if crossed is None else crossed + cross
        slots_of[m * rows : (m + 1) * rows, :] = straight + partners(crossed, bands)
    out_ref[...] = slots_of[...].T


def gains_kernel(slots, where_ref, noise_ref, var_ref, scale_ref, out_ref, var, scale):
    last = var_ref.shape[0] - 1
    var[...] = jnp.ones_like(var)
    scale[...] = jnp.ones_like(scale)
    for m in range(slots):
        row = jnp.minimum(slots * where_ref[0] + m, last)
        var[m : m + 1, :] = var_ref[pl.ds(row, 1), :]
        scale[m : m + 1, :] = scale_ref[pl.ds(row, 1), :]
    variance = var[...]
    rate = ROOT_FIVE / scale[...]
    damping = jnp.exp(-rate)
    a = [
        [
            damping
            * (
                (1.0 if i == j else 0.0)
                + rate * NILPOTENT[i][j]
                + 0.5 * rate * rate * NILPOTENT_SQUARED[i][j]
            )
            for j in range(3)
        ]
        for i in range(3)
    ]
    for i in range(3):
        for j in range(3):
            out_ref[3 * i + j] = a[i][j]

    def carried(cov):
        ap = [[a[i][0] * cov[0][j] + a[i][1] * cov[1][j] + a[i][2] * cov[2][j] for j in range(3)] for i in range(3)]
        upper = {
            (i, j): ap[i][0] * a[j][0] + ap[i][1] * a[j][1] + ap[i][2] * a[j][2]
            for i in range(3)
            for j in range(i, 3)
        }
        return [[upper[min(i, j), max(i, j)] for j in range(3)] for i in range(3)]

    cov = [[variance * STATIONARY[i][j] for j in range(3)] for i in range(3)]
    start = carried(cov)
    noise_cov = [[cov[i][j] - start[i][j] for j in range(3)] for i in range(3)]
    for h in range((out_ref.shape[0] - 9) // 4):
        noise = noise_ref[h]
        moved = carried(cov)
        pm = {(i, j): moved[i][j] + noise_cov[i][j] for i in range(3) for j in range(i, 3)}
        inverse = 1.0 / (pm[0, 0] + noise)
        k = [pm[0, j] * inverse for j in range(3)]
        for j in range(3):
            out_ref[9 + 4 * h + j] = k[j]
        out_ref[9 + 4 * h + 3] = inverse
        first = [noise * k[j] for j in range(3)]
        c11 = pm[1, 1] - k[1] * pm[0, 1]
        c12 = pm[1, 2] - k[1] * pm[0, 2]
        c22 = pm[2, 2] - k[2] * pm[0, 2]
        cov = [[first[0], first[1], first[2]], [first[1], c11, c12], [first[2], c12, c22]]


def smooth_kernel(lats, noise_ref, x_ref, gain_ref, into_ref, back_ref, out_ref, turned, grid, series):
    owners, lanes = x_ref.shape
    hours = (gain_ref.shape[0] - 9) // 4
    bands = grid.shape[1] // lats
    blocks = owners // bands
    per_block = hours // blocks
    stride = per_block * SUB
    parts, _, width = turned.shape
    for part in range(parts):
        turned[part] = x_ref[part * width : (part + 1) * width, :].T
    per_part = width // bands
    for h in range(per_block):
        for lat in range(lats):
            for part in range(parts):
                rows = turned[part, pl.ds(lat * per_block + h, SUB, stride=stride), :]
                for t in range(per_part):
                    at = ((part * per_part + t) * per_block + h) * SUB
                    grid[at : at + SUB, lat * bands : (lat + 1) * bands] = rows[:, t * bands : (t + 1) * bands]
    series[...] = product(grid[...], into_ref[0], into_ref[1])

    a = [[gain_ref[3 * i + j] for j in range(3)] for i in range(3)]
    scaled = []
    mean = None
    for h in range(hours):
        seen = series[h * SUB : (h + 1) * SUB, :]
        if mean is None:
            error = seen
            mean = [gain_ref[9 + 4 * h + j] * error for j in range(3)]
        else:
            ahead = [a[i][0] * mean[0] + a[i][1] * mean[1] + a[i][2] * mean[2] for i in range(3)]
            error = seen - ahead[0]
            mean = [ahead[j] + gain_ref[9 + 4 * h + j] * error for j in range(3)]
        scaled.append(error * gain_ref[9 + 4 * h + 3])
    adjoint = None
    for h in reversed(range(hours)):
        drop = scaled[h]
        if adjoint is not None:
            drop = drop + (gain_ref[9 + 4 * h + 0] * adjoint[0] + gain_ref[9 + 4 * h + 1] * adjoint[1] + gain_ref[9 + 4 * h + 2] * adjoint[2])
        here = slice(h * SUB, (h + 1) * SUB)
        series[here, :] = series[here, :] - noise_ref[h] * drop
        if adjoint is None:
            adjoint = [-(a[0][j] * drop) for j in range(3)]
        else:
            less = adjoint[0] - drop
            adjoint = [a[0][j] * less + a[1][j] * adjoint[1] + a[2][j] * adjoint[2] for j in range(3)]

    grid[...] = product(series[...], back_ref[0], back_ref[1])
    turned[...] = jnp.zeros_like(turned)
    for h in range(per_block):
        for lat in range(lats):
            for part in range(parts):
                rows = jnp.concatenate(
                    [
                        grid[(t * per_block + h) * SUB : (t * per_block + h + 1) * SUB, lat * bands : (lat + 1) * bands]
                        for t in range(part * per_part, (part + 1) * per_part)
                    ],
                    axis=1,
                )
                turned[part, pl.ds(lat * per_block + h, SUB, stride=stride), :] = rows
    for part in range(parts):
        out_ref[part * width : (part + 1) * width, :] = turned[part].T


def synthesise_kernel(bands, x_ref, table_ref, turns_ref, out_ref, turned, flat):
    lats, hours, lon = out_ref.shape
    slots = table_ref.shape[0]
    steps = lon // STEP
    rows = 2 * SUB
    turned[...] = x_ref[...].T
    total = None
    for m in range(slots):
        plain = turned[m * rows : (m + 1) * rows, :]
        cross = partners(plain, bands)
        value = jnp.concatenate(
            [plain * turns_ref[m, 0, b : b + 1, :] + cross * turns_ref[m, 1, b : b + 1, :] for b in range(steps)], axis=0
        )
        part = product(value, table_ref[m, 0], table_ref[m, 1])
        total = part if total is None else total + part
    for b in range(steps):
        flat[:, b * STEP : (b + 1) * STEP] = total[b * rows : (b + 1) * rows, :STEP]
    for lat in range(lats):
        out_ref[lat] = flat[lat * hours : (lat + 1) * hours, :]


def params(mib):
    return pltpu.CompilerParams(vmem_limit_bytes=mib * MIB)


def per_device(tables, observed, noise_var, spectral_var, time_scale):
    lon_into, lon_back, turns, lat_into, lat_back = tables
    hours_dev, lat_dev, lon_size = observed.shape
    hours = noise_var.shape[0]
    bands = lax.axis_size("space")
    slots, _, _, owners = lon_into.shape
    lat_size = lat_into.shape[-1]
    rows = 2 * SUB
    lanes = SUB * rows
    vmem = pl.BlockSpec(memory_space=pltpu.VMEM)
    smem = pl.BlockSpec(memory_space=pltpu.SMEM)
    hbm = pl.BlockSpec(memory_space=pltpu.HBM)

    by_lat = observed.transpose(1, 0, 2)
    sent = pl.pallas_call(
        functools.partial(analyse_kernel, bands),
        out_shape=jax.ShapeDtypeStruct((owners, lanes), F32),
        in_specs=[hbm] * 3,
        out_specs=vmem,
        scratch_shapes=[
            pltpu.VMEM(by_lat.shape, F32),
            pltpu.VMEM(lon_into.shape, BF16),
            pltpu.VMEM(turns.shape, F32),
            pltpu.VMEM((rows, lon_size), F32),
            pltpu.VMEM((lon_size // STEP * rows, LANES), F32),
            pltpu.VMEM((lanes, owners), F32),
            pltpu.SemaphoreType.DMA((2 + slots,)),
        ],
        compiler_params=params(16),
        name="analyse",
    )(*(pltpu.with_memory_space_constraint(each, pltpu.HBM) for each in (by_lat, lon_into, turns)))
    got = lax.all_to_all(sent, ("tm", "space"), split_axis=0, concat_axis=0, tiled=True)

    where = lax.axis_index("tm").astype(jnp.int32).reshape(1)
    gains = pl.pallas_call(
        functools.partial(gains_kernel, slots),
        out_shape=jax.ShapeDtypeStruct((9 + 4 * hours, SUB, lat_size), F32),
        in_specs=[smem, smem, vmem, vmem],
        out_specs=vmem,
        scratch_shapes=[pltpu.VMEM((SUB, lat_size), F32)] * 2,
        cost_estimate=pl.CostEstimate(flops=200 * hours * SUB * 256, bytes_accessed=2 * MIB, transcendentals=0),
        compiler_params=params(8),
        name="gains",
    )(where, noise_var, spectral_var, time_scale)

    smooth = pl.pallas_call(
        functools.partial(smooth_kernel, lat_dev),
        out_shape=jax.ShapeDtypeStruct((owners, lanes), F32),
        in_specs=[smem] + [vmem] * 4,
        out_specs=vmem,
        scratch_shapes=[
            pltpu.VMEM((owners // LANES, lanes, LANES), F32),
            pltpu.VMEM((hours * SUB, lat_size), F32),
            pltpu.VMEM((hours * SUB, lat_size), F32),
        ],
        compiler_params=params(16),
        name="smooth",
    )(noise_var, got, gains, lat_into, lat_back)
    back = lax.all_to_all(smooth, ("tm", "space"), split_axis=0, concat_axis=0, tiled=True)

    field = pl.pallas_call(
        functools.partial(synthesise_kernel, bands),
        out_shape=jax.ShapeDtypeStruct(by_lat.shape, F32),
        in_specs=[vmem] * 3,
        out_specs=vmem,
        scratch_shapes=[pltpu.VMEM((lanes, owners), F32), pltpu.VMEM((rows, lon_size), F32)],
        compiler_params=params(16),
        name="synthesise",
    )(back, lon_back, turns)
    return field.transpose(1, 0, 2)


def solution(mesh):
    placed = (P("tm", "space", None), P(), P("space", None), P("space", None))
    blocks, bands = mesh.shape["tm"], mesh.shape["space"]

    def whole(observed, noise_var, spectral_var, time_scale):
        lon_size = observed.shape[2]
        lat_size = spectral_var.shape[1]
        head, turns = lon_tables(lon_size, blocks, bands)
        by_lat = lat_basis(lat_size).reshape(lat_size, bands, lat_size // bands)
        by_lat = by_lat.transpose(0, 2, 1).reshape(lat_size, lat_size)
        tables = (
            two_halves(head.transpose(0, 2, 1)),
            two_halves(head),
            turns,
            two_halves(by_lat.T),
            two_halves(by_lat),
        )
        tables = tuple(jnp.asarray(table) for table in tables)
        return jax.shard_map(
            functools.partial(per_device, tables),
            mesh=mesh,
            in_specs=placed,
            out_specs=P("tm", "space", None),
            check_vma=False,
        )(observed, noise_var, spectral_var, time_scale)

    return whole
```

time: 62.2 us -> 54.1 us (0.87)
  local copies, waits for them, and re-layouts: 8.15 us -> 0.66 us
  waiting for transfers between devices: 9.93 us -> 11 us
  Pallas kernels: 9.16 us -> 8.18 us
    unnamed x15 -> x14, local copies, waits for them, and re-layouts: 7.43 us -> 0.66 us
    all_to_all x1, waiting for transfers between devices: 9.93 us -> 11 us  [per_device(): lax.all_to_all(sent, ('tm', 'space'), split_axis=0, concat_axis=0, tiled=...]
    pallas_call x3, Pallas kernels: 7.5 us -> 6.5 us  [the longest x1 4 us: per_device(): pl.pallas_call(functools.partial(analyse_kernel, bands), out_shape=jax.Sh...]
    pallas_call x1 -> x0, local copies, waits for them, and re-layouts: 0.72 us -> none  [per_device(): pl.pallas_call(synthesise_kernel, out_shape=jax.ShapeDtypeStruct(observed...]
  transfers between devices with their start and end apart: 1 -> 1, of which waited for: 1 -> 1; matrix products, arithmetic and copies ran while one was open for 1% -> 0% of each run, Pallas kernels for 3% -> 2%
where the time goes in v2:
time: 54.1 us; the launch traced here: 53.9 us
  blocking collectives  18.4 us (34%)
  starting transfers between devices  15.7 us (29%)
  waiting for transfers between devices  11 us (20%)
  Pallas kernels  8.18 us (15%)
  local copies, waits for them, and re-layouts  0.66 us (1%)
    all_to_all x1, blocking collectives, per_device(): lax.all_to_all(smooth, ('tm', 'space'), split_axis=0, concat_axis=0, tile...  18.4 us
    all_to_all x1, starting transfers between devices, per_device(): lax.all_to_all(sent, ('tm', 'space'), split_axis=0, concat_axis=0, tiled=...  15.7 us
    all_to_all x1, waiting for transfers between devices, per_device(): lax.all_to_all(sent, ('tm', 'space'), split_axis=0, concat_axis=0, tiled=...  11 us
    pallas_call x1, Pallas kernels, per_device(): pl.pallas_call(functools.partial(analyse_kernel, bands), out_shape=jax.Sh...  4 us
    pallas_call x1, Pallas kernels, per_device(): pl.pallas_call(functools.partial(smooth_kernel, lat_dev), out_shape=jax.S...  1.68 us
    pallas_call x1, Pallas kernels, per_device(): pl.pallas_call(functools.partial(synthesise_kernel, bands), out_shape=jax...  1.52 us
  transfers between devices with their start and end apart: 1, of which 1 were waited for; matrix products, arithmetic and copies ran while one was open for 0% of the time, Pallas kernels for 2%

profile of v2, /device:TPU:1, one launch (start us, length us, event | category | flops | bytes accessed | tf_op | source)
XLA Modules:
  0.0 53.9 jit_solution(1469276601110885399)
XLA Ops:
  0.0 4.0 %analyse.1 = f32[256,128]{1,0:T(8,128)} custom-call(f32[6,2,1440]{2,1,0:T(2,128)} %bitcast.14, bf16[6,2,128,256]{3,2,1,0:T(8,128)(2,1)} %constant.16.clone.table_hbm, f32[6,2,12,256]{3,2,1,0:T(8,128)} %constant.17.clone.turns_hbm.turns_ref), custom_call_target="tpu_custom_call" | custom-call | tf_op jit(solution)/shard_map/analyse/pallas_call | solution.py:287
  4.0 0.0 copy-start.4
  4.0 0.0 copy-start.5
  4.0 15.7 %all-to-all-start = ((f32[256,1,128]{2,1,0:T(1,128)}), f32[256,1,128]{2,1,0:T(1,128)S(1)}, u32[]{:S(2)}, u32[]{:S(2)}) async-start(f32[256,1,128]{2,1,0:T(1,128)} %bitcast.2), calls=%async_computation | async-start | bytes 262144 | tf_op jit(solution)/shard_map/all_to_all | solution.py:304
  19.7 0.0 copy-start.6
  19.7 0.0 copy-done.4
  19.7 0.0 copy-done.5
  19.7 0.6 %copy-done.6 = f32[16]{0:T(128)S(1)} copy-done((f32[16]{0:T(128)S(1)}, f32[16]{0:T(128)}, u32[]{:S(2)}) %copy-start.6) | copy-done | bytes 88
  20.4 0.0 copy-start.2
  20.4 0.0 copy-start.3
  20.4 1.0 %gains.1.gain_ref = f32[73,8,192]{2,1,0:T(8,128)S(1)} custom-call(s32[1]{0:T(128)} %bitcast.4.where_ref, f32[16]{0:T(128)S(1)} %copy-done.6, f32[45,192]{1,0:T(8,128)S(1)} %copy-done.4, f32[45,192]{1,0:T(8,128)S(1)} %copy-done.5), custom_call_target="tpu_custom_call" | custom-call | flops 6553600 | bytes 2097152 | tf_op jit(solution)/shard_map/gains/pallas_call | solution.py:307
  21.4 0.0 copy-start.1
  21.4 11.0 %all-to-all-done = f32[256,1,128]{2,1,0:T(1,128)S(1)} async-done(((f32[256,1,128]{2,1,0:T(1,128)}), f32[256,1,128]{2,1,0:T(1,128)S(1)}, u32[]{:S(2)}, u32[]{:S(2)}) %all-to-all-start) | async-done | bytes 131104 | tf_op jit(solution)/shard_map/all_to_all | solution.py:304
  32.4 0.0 copy-done.2
  32.4 0.0 copy-done.3
  32.4 1.7 %smooth.1 = f32[256,128]{1,0:T(8,128)S(1)} custom-call(f32[16]{0:T(128)S(1)} %copy-done.6, f32[256,128]{1,0:T(8,128)S(1)} %bitcast.11, f32[73,8,192]{2,1,0:T(8,128)S(1)} %gains.1.gain_ref, bf16[2,192,192]{2,1,0:T(8,128)(2,1)S(1)} %copy-done.3, bf16[2,192,192]{2,1,0:T(8,128)(2,1)S(1)} %copy-done.2), custom_call_target="tpu_custom_call" | custom-call | tf_op jit(solution)/shard_map/smooth/pallas_call | solution.py:318
  34.0 0.0 copy-start
  34.1 18.4 %all_to_all.22 = f32[256,1,128]{2,1,0:T(1,128)S(1)} all-to-all(f32[256,1,128]{2,1,0:T(1,128)S(1)} %bitcast.12), channel_id=1, replica_groups=mesh['tm'=8,'space'=32] {'tm','space'}, dimensions={0} | all-to-all | bytes 262144 | tf_op jit(solution)/shard_map/all_to_all | solution.py:331
  52.4 0.0 copy-done.1
  52.4 0.0 copy-done
  52.4 1.5 %synthesise.1 = f32[6,2,1440]{2,1,0:T(2,128)} custom-call(f32[256,128]{1,0:T(8,128)S(1)} %bitcast.13, bf16[6,2,256,128]{3,2,1,0:T(8,128)(2,1)S(1)} %copy-done.1, f32[6,2,12,256]{3,2,1,0:T(8,128)S(1)} %copy-done), custom_call_target="tpu_custom_call" | custom-call | tf_op jit(solution)/shard_map/synthesise/pallas_call | solution.py:333
Async XLA Ops:
  4.0 15.7 %copy-start.4 = (f32[45,192]{1,0:T(8,128)S(1)}, f32[45,192]{1,0:T(8,128)}, u32[]{:S(2)}) copy-start(f32[45,192]{1,0:T(8,128)} %var_ref.1) | copy-start | bytes 103684
  4.0 15.7 %copy-start.5 = (f32[45,192]{1,0:T(8,128)S(1)}, f32[45,192]{1,0:T(8,128)}, u32[]{:S(2)}) copy-start(f32[45,192]{1,0:T(8,128)} %scale_ref.1) | copy-start | bytes 103684
  4.0 28.3 %all-to-all-start = ((f32[256,1,128]{2,1,0:T(1,128)}), f32[256,1,128]{2,1,0:T(1,128)S(1)}, u32[]{:S(2)}, u32[]{:S(2)}) async-start(f32[256,1,128]{2,1,0:T(1,128)} %bitcast.2), calls=%async_computation | async-start | bytes 262144 | tf_op jit(solution)/shard_map/all_to_all | solution.py:304
  19.7 0.7 %copy-start.6 = (f32[16]{0:T(128)S(1)}, f32[16]{0:T(128)}, u32[]{:S(2)}) copy-start(f32[16]{0:T(128)} %noise_ref.3) | copy-start | bytes 196
  20.4 12.0 %copy-start.2 = (bf16[2,192,192]{2,1,0:T(8,128)(2,1)S(1)}, bf16[2,192,192]{2,1,0:T(8,128)(2,1)}, u32[]{:S(2)}) copy-start(bf16[2,192,192]{2,1,0:T(8,128)(2,1)} %constant.19.clone.back_ref) | copy-start | bytes 442372
  20.4 12.0 %copy-start.3 = (bf16[2,192,192]{2,1,0:T(8,128)(2,1)S(1)}, bf16[2,192,192]{2,1,0:T(8,128)(2,1)}, u32[]{:S(2)}) copy-start(bf16[2,192,192]{2,1,0:T(8,128)(2,1)} %constant.18.clone.into_ref) | copy-start | bytes 442372
  21.4 31.1 %copy-start.1 = (bf16[6,2,256,128]{3,2,1,0:T(8,128)(2,1)S(1)}, bf16[6,2,256,128]{3,2,1,0:T(8,128)(2,1)}, u32[]{:S(2)}) copy-start(bf16[6,2,256,128]{3,2,1,0:T(8,128)(2,1)} %constant.20.clone.table_ref) | copy-start | bytes 2359300
  34.0 18.4 %copy-start = (f32[6,2,12,256]{3,2,1,0:T(8,128)S(1)}, f32[6,2,12,256]{3,2,1,0:T(8,128)}, u32[]{:S(2)}) copy-start(f32[6,2,12,256]{3,2,1,0:T(8,128)} %constant.17.clone.turns_hbm.turns_ref) | copy-start | bytes 442372

commit v3 on v2

--- a/solution.py
+++ b/solution.py
@@ -95,13 +95,12 @@
     slots = table.shape[0]
     steps = lon // STEP
     rows = 2 * SUB
-    fetch = [pltpu.make_async_copy(x_hbm, x, sems.at[0]), pltpu.make_async_copy(turns_hbm, turns, sems.at[1])]
-    fetch += [pltpu.make_async_copy(table_hbm.at[m], table.at[m], sems.at[2 + m]) for m in range(slots)]
-    fetch[0].start()
-    fetch[2].start()
-    fetch[1].start()
-    for m in range(1, slots):
-        fetch[2 + m].start()
+    fetch = [
+        pltpu.make_async_copy(here, there, sems.at[i])
+        for i, (here, there) in enumerate(((x_hbm, x), (table_hbm, table), (turns_hbm, turns)))
+    ]
+    for copy in fetch:
+        copy.start()
     flat[...] = jnp.zeros_like(flat)
     blocks[...] = jnp.zeros_like(blocks)
     slots_of[...] = jnp.zeros_like(slots_of)
@@ -112,10 +111,11 @@
         blocks[b * rows : (b + 1) * rows, :STEP] = flat[:, b * STEP : (b + 1) * STEP]
     value = blocks[...]
     for m in range(slots):
-        fetch[2 + m].wait()
+        if m == 0:
+            fetch[1].wait()
         part = product(value, table[m, 0], table[m, 1])
         if m == 0:
-            fetch[1].wait()
+            fetch[2].wait()
         straight = crossed = None
         for b in range(steps):
             here = part[b * rows : (b + 1) * rows]
@@ -296,7 +296,7 @@
             pltpu.VMEM((rows, lon_size), F32),
             pltpu.VMEM((lon_size // STEP * rows, LANES), F32),
             pltpu.VMEM((lanes, owners), F32),
-            pltpu.SemaphoreType.DMA((2 + slots,)),
+            pltpu.SemaphoreType.DMA((3,)),
         ],
         compiler_params=params(16),
         name="analyse",

time: 54.1 us -> 53.1 us (0.982)
  Pallas kernels: 8.18 us -> 7.08 us
    pallas_call x1, Pallas kernels: 4 us -> 2.89 us  [per_device(): pl.pallas_call(functools.partial(analyse_kernel, bands), out_shape=jax.Sh...]
where the time goes in v3:
time: 53.1 us; the launch traced here: 52.8 us
  blocking collectives  18.4 us (35%)
  starting transfers between devices  15.7 us (30%)
  waiting for transfers between devices  11 us (21%)
  Pallas kernels  7.08 us (13%)
  local copies, waits for them, and re-layouts  0.66 us (1%)
    all_to_all x1, blocking collectives, per_device(): lax.all_to_all(smooth, ('tm', 'space'), split_axis=0, concat_axis=0, tile...  18.4 us
    all_to_all x1, starting transfers between devices, per_device(): lax.all_to_all(sent, ('tm', 'space'), split_axis=0, concat_axis=0, tiled=...  15.7 us
    all_to_all x1, waiting for transfers between devices, per_device(): lax.all_to_all(sent, ('tm', 'space'), split_axis=0, concat_axis=0, tiled=...  11 us
    pallas_call x1, Pallas kernels, per_device(): pl.pallas_call(functools.partial(analyse_kernel, bands), out_shape=jax.Sh...  2.89 us
    pallas_call x1, Pallas kernels, per_device(): pl.pallas_call(functools.partial(smooth_kernel, lat_dev), out_shape=jax.S...  1.68 us
    pallas_call x1, Pallas kernels, per_device(): pl.pallas_call(functools.partial(synthesise_kernel, bands), out_shape=jax...  1.53 us
  transfers between devices with their start and end apart: 1, of which 1 were waited for; matrix products, arithmetic and copies ran while one was open for 0% of the time, Pallas kernels for 2%

profile of v3, /device:TPU:1, one launch (start us, length us, event | category | flops | bytes accessed | tf_op | source)
XLA Modules:
  0.0 52.8 jit_solution(15174396472733211866)
XLA Ops:
  0.0 2.9 %analyse.1 = f32[256,128]{1,0:T(8,128)} custom-call(f32[6,2,1440]{2,1,0:T(2,128)} %bitcast.14, bf16[6,2,128,256]{3,2,1,0:T(8,128)(2,1)} %constant.16.clone.table_hbm, f32[6,2,12,256]{3,2,1,0:T(8,128)} %constant.17.clone.turns_hbm.turns_ref), custom_call_target="tpu_custom_call" | custom-call | tf_op jit(solution)/shard_map/analyse/pallas_call | solution.py:287
  2.9 0.0 copy-start.4
  2.9 0.0 copy-start.5
  2.9 15.7 %all-to-all-start = ((f32[256,1,128]{2,1,0:T(1,128)}), f32[256,1,128]{2,1,0:T(1,128)S(1)}, u32[]{:S(2)}, u32[]{:S(2)}) async-start(f32[256,1,128]{2,1,0:T(1,128)} %bitcast.2), calls=%async_computation | async-start | bytes 262144 | tf_op jit(solution)/shard_map/all_to_all | solution.py:304
  18.6 0.0 copy-start.6
  18.6 0.0 copy-done.4
  18.6 0.0 copy-done.5
  18.6 0.6 %copy-done.6 = f32[16]{0:T(128)S(1)} copy-done((f32[16]{0:T(128)S(1)}, f32[16]{0:T(128)}, u32[]{:S(2)}) %copy-start.6) | copy-done | bytes 88
  19.3 0.0 copy-start.2
  19.3 0.0 copy-start.3
  19.3 1.0 %gains.1.gain_ref = f32[73,8,192]{2,1,0:T(8,128)S(1)} custom-call(s32[1]{0:T(128)} %bitcast.4.where_ref, f32[16]{0:T(128)S(1)} %copy-done.6, f32[45,192]{1,0:T(8,128)S(1)} %copy-done.4, f32[45,192]{1,0:T(8,128)S(1)} %copy-done.5), custom_call_target="tpu_custom_call" | custom-call | flops 6553600 | bytes 2097152 | tf_op jit(solution)/shard_map/gains/pallas_call | solution.py:307
  20.3 0.0 copy-start.1
  20.3 11.0 %all-to-all-done = f32[256,1,128]{2,1,0:T(1,128)S(1)} async-done(((f32[256,1,128]{2,1,0:T(1,128)}), f32[256,1,128]{2,1,0:T(1,128)S(1)}, u32[]{:S(2)}, u32[]{:S(2)}) %all-to-all-start) | async-done | bytes 131104 | tf_op jit(solution)/shard_map/all_to_all | solution.py:304
  31.2 0.0 copy-done.2
  31.2 0.0 copy-done.3
  31.3 1.7 %smooth.1 = f32[256,128]{1,0:T(8,128)S(1)} custom-call(f32[16]{0:T(128)S(1)} %copy-done.6, f32[256,128]{1,0:T(8,128)S(1)} %bitcast.11, f32[73,8,192]{2,1,0:T(8,128)S(1)} %gains.1.gain_ref, bf16[2,192,192]{2,1,0:T(8,128)(2,1)S(1)} %copy-done.3, bf16[2,192,192]{2,1,0:T(8,128)(2,1)S(1)} %copy-done.2), custom_call_target="tpu_custom_call" | custom-call | tf_op jit(solution)/shard_map/smooth/pallas_call | solution.py:318
  32.9 0.0 copy-start
  32.9 18.4 %all_to_all.22 = f32[256,1,128]{2,1,0:T(1,128)S(1)} all-to-all(f32[256,1,128]{2,1,0:T(1,128)S(1)} %bitcast.12), channel_id=1, replica_groups=mesh['tm'=8,'space'=32] {'tm','space'}, dimensions={0} | all-to-all | bytes 262144 | tf_op jit(solution)/shard_map/all_to_all | solution.py:331
  51.3 0.0 copy-done.1
  51.3 0.0 copy-done
  51.3 1.5 %synthesise.1 = f32[6,2,1440]{2,1,0:T(2,128)} custom-call(f32[256,128]{1,0:T(8,128)S(1)} %bitcast.13, bf16[6,2,256,128]{3,2,1,0:T(8,128)(2,1)S(1)} %copy-done.1, f32[6,2,12,256]{3,2,1,0:T(8,128)S(1)} %copy-done), custom_call_target="tpu_custom_call" | custom-call | tf_op jit(solution)/shard_map/synthesise/pallas_call | solution.py:333
Async XLA Ops:
  2.9 15.7 %copy-start.4 = (f32[45,192]{1,0:T(8,128)S(1)}, f32[45,192]{1,0:T(8,128)}, u32[]{:S(2)}) copy-start(f32[45,192]{1,0:T(8,128)} %var_ref.1) | copy-start | bytes 103684
  2.9 15.7 %copy-start.5 = (f32[45,192]{1,0:T(8,128)S(1)}, f32[45,192]{1,0:T(8,128)}, u32[]{:S(2)}) copy-start(f32[45,192]{1,0:T(8,128)} %scale_ref.1) | copy-start | bytes 103684
  2.9 28.3 %all-to-all-start = ((f32[256,1,128]{2,1,0:T(1,128)}), f32[256,1,128]{2,1,0:T(1,128)S(1)}, u32[]{:S(2)}, u32[]{:S(2)}) async-start(f32[256,1,128]{2,1,0:T(1,128)} %bitcast.2), calls=%async_computation | async-start | bytes 262144 | tf_op jit(solution)/shard_map/all_to_all | solution.py:304
  18.6 0.7 %copy-start.6 = (f32[16]{0:T(128)S(1)}, f32[16]{0:T(128)}, u32[]{:S(2)}) copy-start(f32[16]{0:T(128)} %noise_ref.3) | copy-start | bytes 196
  19.3 12.0 %copy-start.2 = (bf16[2,192,192]{2,1,0:T(8,128)(2,1)S(1)}, bf16[2,192,192]{2,1,0:T(8,128)(2,1)}, u32[]{:S(2)}) copy-start(bf16[2,192,192]{2,1,0:T(8,128)(2,1)} %constant.19.clone.back_ref) | copy-start | bytes 442372
  19.3 12.0 %copy-start.3 = (bf16[2,192,192]{2,1,0:T(8,128)(2,1)S(1)}, bf16[2,192,192]{2,1,0:T(8,128)(2,1)}, u32[]{:S(2)}) copy-start(bf16[2,192,192]{2,1,0:T(8,128)(2,1)} %constant.18.clone.into_ref) | copy-start | bytes 442372
  20.3 31.1 %copy-start.1 = (bf16[6,2,256,128]{3,2,1,0:T(8,128)(2,1)S(1)}, bf16[6,2,256,128]{3,2,1,0:T(8,128)(2,1)}, u32[]{:S(2)}) copy-start(bf16[6,2,256,128]{3,2,1,0:T(8,128)(2,1)} %constant.20.clone.table_ref) | copy-start | bytes 2359300
  32.9 18.4 %copy-start = (f32[6,2,12,256]{3,2,1,0:T(8,128)S(1)}, f32[6,2,12,256]{3,2,1,0:T(8,128)}, u32[]{:S(2)}) copy-start(f32[6,2,12,256]{3,2,1,0:T(8,128)} %constant.17.clone.turns_hbm.turns_ref) | copy-start | bytes 442372

commit v4 on v3

--- a/solution.py
+++ b/solution.py
@@ -19,13 +19,14 @@
 SUB = 8
 LANES = 128
 STEP = 120
+STEP_BACK = 240
 MIB = 2**20
 
 
-def two_halves(table):
+def stacked(table):
     high = table.astype(ml_dtypes.bfloat16)
     low = (table - high.astype(np.float64)).astype(ml_dtypes.bfloat16)
-    return np.stack([high, low], axis=-3)
+    return np.concatenate([high, high, low], axis=-2)
 
 
 def lon_basis(size):
@@ -47,7 +48,7 @@
     return np.cos(radians) * weight
 
 
-def lon_tables(size, hour_blocks, bands):
+def lon_tables(size, step, hour_blocks, bands):
     per_band = size // bands
     slots = -(-per_band // hour_blocks)
     half = size // 2
@@ -60,15 +61,28 @@
     rows = (lon_basis(size)[mode] * used[..., None]).reshape(slots, hour_blocks * bands, size)
     sine = mode > half
     frequency = np.where(sine, mode - half, mode)
-    ahead = np.arange(size // STEP)[:, None, None, None] * STEP
+    ahead = np.arange(size // step)[:, None, None, None] * step
     radians = (frequency * ahead % size) * (2.0 * math.pi / size)
     straight = np.where(used, np.cos(radians), 0.0)
     crossed = np.where(used & (mode % half != 0), np.sin(radians), 0.0) * np.where(sine, 1.0, -1.0)
     crossed = np.roll(crossed, bands // 2, axis=-1)
-    turns = np.stack([straight, crossed]).reshape(2, size // STEP, slots, hour_blocks * bands)
-    head = np.zeros((slots, hour_blocks * bands, LANES))
-    head[..., :STEP] = rows[..., :STEP]
+    turns = np.stack([straight, crossed]).reshape(2, size // step, slots, hour_blocks * bands)
+    head = np.zeros((slots, hour_blocks * bands, -(-step // LANES) * LANES))
+    head[..., :step] = rows[..., :step]
     return head, turns.transpose(2, 0, 1, 3).astype(np.float32)
+
+
+def all_tables(lon_size, lat_size, blocks, bands):
+    head, turns = lon_tables(lon_size, STEP, blocks, bands)
+    slots, owners, _ = head.shape
+    into = np.concatenate([head[..., :STEP].transpose(0, 2, 1), turns.reshape(slots, -1, owners)], axis=1)
+    head, turns = lon_tables(lon_size, STEP_BACK, blocks, bands)
+    back = stacked(head).reshape(-1, head.shape[-1])
+    by_lat = lat_basis(lat_size).reshape(lat_size, bands, lat_size // bands)
+    by_lat = by_lat.transpose(0, 2, 1).reshape(lat_size, lat_size)
+    pad = -lat_size % (2 * LANES)
+    by_lat = np.pad(by_lat, ((0, pad), (0, pad)))
+    return into.astype(np.float32), back, turns, stacked(by_lat.T), stacked(by_lat)
 
 
 def split(value):
@@ -76,11 +90,13 @@
     return high, (value - high.astype(F32)).astype(BF16)
 
 
-def product(value, table_high, table_low):
-    rows = value.shape[0]
+def spread(value):
     high, low = split(value)
-    both = jnp.dot(jnp.concatenate([high, low], axis=0), table_high, preferred_element_type=F32)
-    return both[:rows] + both[rows:] + jnp.dot(high, table_low, preferred_element_type=F32)
+    return jnp.concatenate([high, low, high], axis=1)
+
+
+def product(value, table):
+    return jnp.dot(spread(value), table, preferred_element_type=F32)
 
 
 def partners(value, bands):
@@ -90,15 +106,12 @@
     return jnp.where(upper, pltpu.roll(value, half, 1), pltpu.roll(value, width - half, 1))
 
 
-def analyse_kernel(bands, x_hbm, table_hbm, turns_hbm, out_ref, x, table, turns, flat, blocks, slots_of, sems):
+def analyse_kernel(bands, x_hbm, table_hbm, out_ref, x, table, flat, blocks, slots_of, sems):
     lats, hours, lon = x.shape
     slots = table.shape[0]
     steps = lon // STEP
     rows = 2 * SUB
-    fetch = [
-        pltpu.make_async_copy(here, there, sems.at[i])
-        for i, (here, there) in enumerate(((x_hbm, x), (table_hbm, table), (turns_hbm, turns)))
-    ]
+    fetch = [pltpu.make_async_copy(x_hbm, x, sems.at[0]), pltpu.make_async_copy(table_hbm, table, sems.at[1])]
     for copy in fetch:
         copy.start()
     flat[...] = jnp.zeros_like(flat)
@@ -109,18 +122,16 @@
         flat[lat * hours : (lat + 1) * hours, :] = x[lat]
     for b in range(steps):
         blocks[b * rows : (b + 1) * rows, :STEP] = flat[:, b * STEP : (b + 1) * STEP]
-    value = blocks[...]
+    value = spread(blocks[...])
+    fetch[1].wait()
     for m in range(slots):
-        if m == 0:
-            fetch[1].wait()
-        part = product(value, table[m, 0], table[m, 1])
-        if m == 0:
-            fetch[2].wait()
+        high, low = split(table[m, :LANES, :])
+        part = jnp.dot(value, jnp.concatenate([high, high, low], axis=0), preferred_element_type=F32)
         straight = crossed = None
         for b in range(steps):
             here = part[b * rows : (b + 1) * rows]
-            plain = here * turns[m, 0, b : b + 1, :]
-            cross = here * turns[m, 1, b : b + 1, :]
+            plain = here * table[m, STEP + b : STEP + b + 1, :]
+            cross = here * table[m, STEP + steps + b : STEP + steps + b + 1, :]
             straight = plain if straight is None else straight + plain
             crossed = cross if crossed is None else crossed + cross
         slots_of[m * rows : (m + 1) * rows, :] = straight + partners(crossed, bands)
@@ -133,8 +144,8 @@
     scale[...] = jnp.ones_like(scale)
     for m in range(slots):
         row = jnp.minimum(slots * where_ref[0] + m, last)
-        var[m : m + 1, :] = var_ref[pl.ds(row, 1), :]
-        scale[m : m + 1, :] = scale_ref[pl.ds(row, 1), :]
+        var[m : m + 1, : var_ref.shape[1]] = var_ref[pl.ds(row, 1), :]
+        scale[m : m + 1, : var_ref.shape[1]] = scale_ref[pl.ds(row, 1), :]
     variance = var[...]
     rate = ROOT_FIVE / scale[...]
     damping = jnp.exp(-rate)
@@ -182,10 +193,9 @@
         cov = [[first[0], first[1], first[2]], [first[1], c11, c12], [first[2], c12, c22]]
 
 
-def smooth_kernel(lats, noise_ref, x_ref, gain_ref, into_ref, back_ref, out_ref, turned, grid, series):
+def smooth_kernel(lats, bands, noise_ref, x_ref, gain_ref, into_ref, back_ref, out_ref, turned, grid, series):
     owners, lanes = x_ref.shape
     hours = (gain_ref.shape[0] - 9) // 4
-    bands = grid.shape[1] // lats
     blocks = owners // bands
     per_block = hours // blocks
     stride = per_block * SUB
@@ -193,6 +203,7 @@
     for part in range(parts):
         turned[part] = x_ref[part * width : (part + 1) * width, :].T
     per_part = width // bands
+    grid[:, lats * bands :] = jnp.zeros((grid.shape[0], grid.shape[1] - lats * bands), F32)
     for h in range(per_block):
         for lat in range(lats):
             for part in range(parts):
@@ -200,7 +211,7 @@
                 for t in range(per_part):
                     at = ((part * per_part + t) * per_block + h) * SUB
                     grid[at : at + SUB, lat * bands : (lat + 1) * bands] = rows[:, t * bands : (t + 1) * bands]
-    series[...] = product(grid[...], into_ref[0], into_ref[1])
+    series[...] = product(grid[...], into_ref[...])
 
     a = [[gain_ref[3 * i + j] for j in range(3)] for i in range(3)]
     scaled = []
@@ -228,7 +239,7 @@
             less = adjoint[0] - drop
             adjoint = [a[0][j] * less + a[1][j] * adjoint[1] + a[2][j] * adjoint[2] for j in range(3)]
 
-    grid[...] = product(series[...], back_ref[0], back_ref[1])
+    grid[...] = product(series[...], back_ref[...])
     turned[...] = jnp.zeros_like(turned)
     for h in range(per_block):
         for lat in range(lats):
@@ -247,21 +258,21 @@
 
 def synthesise_kernel(bands, x_ref, table_ref, turns_ref, out_ref, turned, flat):
     lats, hours, lon = out_ref.shape
-    slots = table_ref.shape[0]
-    steps = lon // STEP
+    slots = turns_ref.shape[0]
+    steps = lon // STEP_BACK
     rows = 2 * SUB
     turned[...] = x_ref[...].T
-    total = None
+    values = []
     for m in range(slots):
         plain = turned[m * rows : (m + 1) * rows, :]
         cross = partners(plain, bands)
-        value = jnp.concatenate(
-            [plain * turns_ref[m, 0, b : b + 1, :] + cross * turns_ref[m, 1, b : b + 1, :] for b in range(steps)], axis=0
-        )
-        part = product(value, table_ref[m, 0], table_ref[m, 1])
-        total = part if total is None else total + part
+        turned_on = [
+            plain * turns_ref[m, 0, b : b + 1, :] + cross * turns_ref[m, 1, b : b + 1, :] for b in range(steps)
+        ]
+        values.append(spread(jnp.concatenate(turned_on, axis=0)))
+    total = jnp.dot(jnp.concatenate(values, axis=1), table_ref[...], preferred_element_type=F32)
     for b in range(steps):
-        flat[:, b * STEP : (b + 1) * STEP] = total[b * rows : (b + 1) * rows, :STEP]
+        flat[:, b * STEP_BACK : (b + 1) * STEP_BACK] = total[b * rows : (b + 1) * rows, :STEP_BACK]
     for lat in range(lats):
         out_ref[lat] = flat[lat * hours : (lat + 1) * hours, :]
 
@@ -275,8 +286,8 @@
     hours_dev, lat_dev, lon_size = observed.shape
     hours = noise_var.shape[0]
     bands = lax.axis_size("space")
-    slots, _, _, owners = lon_into.shape
-    lat_size = lat_into.shape[-1]
+    slots, _, owners = lon_into.shape
+    lat_pad = lat_into.shape[-1]
     rows = 2 * SUB
     lanes = SUB * rows
     vmem = pl.BlockSpec(memory_space=pltpu.VMEM)
@@ -287,43 +298,42 @@
     sent = pl.pallas_call(
         functools.partial(analyse_kernel, bands),
         out_shape=jax.ShapeDtypeStruct((owners, lanes), F32),
-        in_specs=[hbm] * 3,
+        in_specs=[hbm] * 2,
         out_specs=vmem,
         scratch_shapes=[
             pltpu.VMEM(by_lat.shape, F32),
-            pltpu.VMEM(lon_into.shape, BF16),
-            pltpu.VMEM(turns.shape, F32),
+            pltpu.VMEM(lon_into.shape, F32),
             pltpu.VMEM((rows, lon_size), F32),
             pltpu.VMEM((lon_size // STEP * rows, LANES), F32),
             pltpu.VMEM((lanes, owners), F32),
-            pltpu.SemaphoreType.DMA((3,)),
+            pltpu.SemaphoreType.DMA((2,)),
         ],
         compiler_params=params(16),
         name="analyse",
-    )(*(pltpu.with_memory_space_constraint(each, pltpu.HBM) for each in (by_lat, lon_into, turns)))
+    )(*(pltpu.with_memory_space_constraint(each, pltpu.HBM) for each in (by_lat, lon_into)))
     got = lax.all_to_all(sent, ("tm", "space"), split_axis=0, concat_axis=0, tiled=True)
 
     where = lax.axis_index("tm").astype(jnp.int32).reshape(1)
     gains = pl.pallas_call(
         functools.partial(gains_kernel, slots),
-        out_shape=jax.ShapeDtypeStruct((9 + 4 * hours, SUB, lat_size), F32),
+        out_shape=jax.ShapeDtypeStruct((9 + 4 * hours, SUB, lat_pad), F32),
         in_specs=[smem, smem, vmem, vmem],
         out_specs=vmem,
-        scratch_shapes=[pltpu.VMEM((SUB, lat_size), F32)] * 2,
+        scratch_shapes=[pltpu.VMEM((SUB, lat_pad), F32)] * 2,
         cost_estimate=pl.CostEstimate(flops=200 * hours * SUB * 256, bytes_accessed=2 * MIB, transcendentals=0),
         compiler_params=params(8),
         name="gains",
     )(where, noise_var, spectral_var, time_scale)
 
     smooth = pl.pallas_call(
-        functools.partial(smooth_kernel, lat_dev),
+        functools.partial(smooth_kernel, lat_dev, bands),
         out_shape=jax.ShapeDtypeStruct((owners, lanes), F32),
         in_specs=[smem] + [vmem] * 4,
         out_specs=vmem,
         scratch_shapes=[
             pltpu.VMEM((owners // LANES, lanes, LANES), F32),
-            pltpu.VMEM((hours * SUB, lat_size), F32),
-            pltpu.VMEM((hours * SUB, lat_size), F32),
+            pltpu.VMEM((hours * SUB, lat_pad), F32),
+            pltpu.VMEM((hours * SUB, lat_pad), F32),
         ],
         compiler_params=params(16),
         name="smooth",
@@ -349,16 +359,7 @@
     def whole(observed, noise_var, spectral_var, time_scale):
         lon_size = observed.shape[2]
         lat_size = spectral_var.shape[1]
-        head, turns = lon_tables(lon_size, blocks, bands)
-        by_lat = lat_basis(lat_size).reshape(lat_size, bands, lat_size // bands)
-        by_lat = by_lat.transpose(0, 2, 1).reshape(lat_size, lat_size)
-        tables = (
-            two_halves(head.transpose(0, 2, 1)),
-            two_halves(head),
-            turns,
-            two_halves(by_lat.T),
-            two_halves(by_lat),
-        )
+        tables = all_tables(observed.shape[2], spectral_var.shape[1], blocks, bands)
         tables = tuple(jnp.asarray(table) for table in tables)
         return jax.shard_map(
             functools.partial(per_device, tables),

time: 53.1 us -> 56.2 us (1.058)
  local copies, waits for them, and re-layouts: 0.66 us -> 5.79 us
  waiting for transfers between devices: 11 us -> 9.38 us
    unnamed x14 -> x16, local copies, waits for them, and re-layouts: 0.66 us -> 5.79 us
    all_to_all x1, waiting for transfers between devices: 11 us -> 9.38 us  [per_device(): lax.all_to_all(sent, ('tm', 'space'), split_axis=0, concat_axis=0, tiled=...]
where the time goes in v4:
time: 56.2 us; the launch traced here: 55.8 us
  blocking collectives  18.3 us (33%)
  starting transfers between devices  15.7 us (28%)
  waiting for transfers between devices  9.38 us (17%)
  Pallas kernels  6.65 us (12%)
  local copies, waits for them, and re-layouts  5.79 us (10%)
    all_to_all x1, blocking collectives, per_device(): lax.all_to_all(smooth, ('tm', 'space'), split_axis=0, concat_axis=0, tile...  18.3 us
    all_to_all x1, starting transfers between devices, per_device(): lax.all_to_all(sent, ('tm', 'space'), split_axis=0, concat_axis=0, tiled=...  15.7 us
    all_to_all x1, waiting for transfers between devices, per_device(): lax.all_to_all(sent, ('tm', 'space'), split_axis=0, concat_axis=0, tiled=...  9.38 us
    unnamed x16, local copies, waits for them, and re-layouts  5.79 us
    pallas_call x1, Pallas kernels, per_device(): pl.pallas_call(functools.partial(analyse_kernel, bands), out_shape=jax.Sh...  2.65 us
    pallas_call x1, Pallas kernels, per_device(): pl.pallas_call(functools.partial(smooth_kernel, lat_dev, bands), out_shap...  1.65 us
    pallas_call x1, Pallas kernels, per_device(): pl.pallas_call(functools.partial(synthesise_kernel, bands), out_shape=jax...  1.37 us
  transfers between devices with their start and end apart: 1, of which 1 were waited for; matrix products, arithmetic and copies ran while one was open for 0% of the time, Pallas kernels for 2%

profile of v4, /device:TPU:1, one launch (start us, length us, event | category | flops | bytes accessed | tf_op | source)
XLA Modules:
  0.0 55.8 jit_solution(12250884821252698193)
XLA Ops:
  0.0 0.0 copy-start
  0.0 2.7 %analyse.1 = f32[256,128]{1,0:T(8,128)} custom-call(f32[6,2,1440]{2,1,0:T(2,128)} %bitcast.14, f32[6,144,256]{2,1,0:T(8,128)} %constant.16.clone.table_hbm), custom_call_target="tpu_custom_call" | custom-call | tf_op jit(solution)/shard_map/analyse/pallas_call | solution.py:298
  2.7 15.7 %all-to-all-start = ((f32[256,1,128]{2,1,0:T(1,128)}), f32[256,1,128]{2,1,0:T(1,128)S(1)}, u32[]{:S(2)}, u32[]{:S(2)}) async-start(f32[256,1,128]{2,1,0:T(1,128)} %bitcast.2), calls=%async_computation | async-start | bytes 262144 | tf_op jit(solution)/shard_map/all_to_all | solution.py:314
  18.3 0.0 copy-start.4
  18.4 0.8 %copy-done.4 = f32[45,192]{1,0:T(8,128)S(1)} copy-done((f32[45,192]{1,0:T(8,128)S(1)}, f32[45,192]{1,0:T(8,128)}, u32[]{:S(2)}) %copy-start.4) | copy-done | bytes 34584
  19.1 0.0 copy-start.5
  19.1 0.8 %copy-done.5 = f32[45,192]{1,0:T(8,128)S(1)} copy-done((f32[45,192]{1,0:T(8,128)S(1)}, f32[45,192]{1,0:T(8,128)}, u32[]{:S(2)}) %copy-start.5) | copy-done | bytes 34584
  19.9 0.0 copy-start.6
  19.9 0.7 %copy-done.6 = f32[16]{0:T(128)S(1)} copy-done((f32[16]{0:T(128)S(1)}, f32[16]{0:T(128)}, u32[]{:S(2)}) %copy-start.6) | copy-done | bytes 88
  20.6 1.0 %gains.1.gain_ref = f32[73,8,256]{2,1,0:T(8,128)S(1)} custom-call(s32[1]{0:T(128)} %bitcast.4.where_ref, f32[16]{0:T(128)S(1)} %copy-done.6, f32[45,192]{1,0:T(8,128)S(1)} %copy-done.4, f32[45,192]{1,0:T(8,128)S(1)} %copy-done.5), custom_call_target="tpu_custom_call" | custom-call | flops 6553600 | bytes 2097152 | tf_op jit(solution)/shard_map/gains/pallas_call | solution.py:317
  21.6 9.4 %all-to-all-done = f32[256,1,128]{2,1,0:T(1,128)S(1)} async-done(((f32[256,1,128]{2,1,0:T(1,128)}), f32[256,1,128]{2,1,0:T(1,128)S(1)}, u32[]{:S(2)}, u32[]{:S(2)}) %all-to-all-start) | async-done | bytes 131104 | tf_op jit(solution)/shard_map/all_to_all | solution.py:314
  31.0 0.0 copy-start.1
  31.0 1.0 %copy-done.1 = bf16[768,256]{1,0:T(8,128)(2,1)S(1)} copy-done((bf16[768,256]{1,0:T(8,128)(2,1)S(1)}, bf16[768,256]{1,0:T(8,128)(2,1)}, u32[]{:S(2)}) %copy-start.1) | copy-done | bytes 393240
  32.0 0.0 copy-start.2
  32.0 1.0 %copy-done.2 = bf16[768,256]{1,0:T(8,128)(2,1)S(1)} copy-done((bf16[768,256]{1,0:T(8,128)(2,1)S(1)}, bf16[768,256]{1,0:T(8,128)(2,1)}, u32[]{:S(2)}) %copy-start.2) | copy-done | bytes 393240
  33.0 0.0 copy-start.7
  33.0 0.7 %copy-done.7 = f32[16]{0:T(128)S(1)} copy-done((f32[16]{0:T(128)S(1)}, f32[16]{0:T(128)}, u32[]{:S(2)}) %copy-start.7) | copy-done | bytes 88
  33.6 1.6 %smooth.1 = f32[256,128]{1,0:T(8,128)S(1)} custom-call(f32[16]{0:T(128)S(1)} %copy-done.7, f32[256,128]{1,0:T(8,128)S(1)} %bitcast.11, f32[73,8,256]{2,1,0:T(8,128)S(1)} %gains.1.gain_ref, bf16[768,256]{1,0:T(8,128)(2,1)S(1)} %copy-done.2, bf16[768,256]{1,0:T(8,128)(2,1)S(1)} %copy-done.1), custom_call_target="tpu_custom_call" | custom-call | tf_op jit(solution)/shard_map/smooth/pallas_call | solution.py:328
  35.3 18.3 %all_to_all.22 = f32[256,1,128]{2,1,0:T(1,128)S(1)} all-to-all(f32[256,1,128]{2,1,0:T(1,128)S(1)} %bitcast.12), channel_id=1, replica_groups=mesh['tm'=8,'space'=32] {'tm','space'}, dimensions={0} | all-to-all | bytes 262144 | tf_op jit(solution)/shard_map/all_to_all | solution.py:341
  53.5 0.0 copy-done
  53.5 0.0 copy-start.3
  53.5 0.9 %copy-done.3 = f32[6,2,6,256]{3,2,1,0:T(8,128)S(1)} copy-done((f32[6,2,6,256]{3,2,1,0:T(8,128)S(1)}, f32[6,2,6,256]{3,2,1,0:T(8,128)}, u32[]{:S(2)}) %copy-start.3) | copy-done | bytes 73752
  54.4 1.4 %synthesise.1 = f32[6,2,1440]{2,1,0:T(2,128)} custom-call(f32[256,128]{1,0:T(8,128)S(1)} %bitcast.13, bf16[4608,256]{1,0:T(8,128)(2,1)S(1)} %copy-done, f32[6,2,6,256]{3,2,1,0:T(8,128)S(1)} %copy-done.3), custom_call_target="tpu_custom_call" | custom-call | tf_op jit(solution)/shard_map/synthesise/pallas_call | solution.py:343
Async XLA Ops:
  0.0 53.5 %copy-start = (bf16[4608,256]{1,0:T(8,128)(2,1)S(1)}, bf16[4608,256]{1,0:T(8,128)(2,1)}, u32[]{:S(2)}) copy-start(bf16[4608,256]{1,0:T(8,128)(2,1)} %constant.19.clone.table_ref) | copy-start | bytes 7077892
  2.7 28.3 %all-to-all-start = ((f32[256,1,128]{2,1,0:T(1,128)}), f32[256,1,128]{2,1,0:T(1,128)S(1)}, u32[]{:S(2)}, u32[]{:S(2)}) async-start(f32[256,1,128]{2,1,0:T(1,128)} %bitcast.2), calls=%async_computation | async-start | bytes 262144 | tf_op jit(solution)/shard_map/all_to_all | solution.py:314
  18.3 0.8 %copy-start.4 = (f32[45,192]{1,0:T(8,128)S(1)}, f32[45,192]{1,0:T(8,128)}, u32[]{:S(2)}) copy-start(f32[45,192]{1,0:T(8,128)} %var_ref.1) | copy-start | bytes 103684
  19.1 0.8 %copy-start.5 = (f32[45,192]{1,0:T(8,128)S(1)}, f32[45,192]{1,0:T(8,128)}, u32[]{:S(2)}) copy-start(f32[45,192]{1,0:T(8,128)} %scale_ref.1) | copy-start | bytes 103684
  19.9 0.7 %copy-start.6 = (f32[16]{0:T(128)S(1)}, f32[16]{0:T(128)}, u32[]{:S(2)}) copy-start(f32[16]{0:T(128)} %noise_ref.3) | copy-start | bytes 196
  31.0 1.0 %copy-start.1 = (bf16[768,256]{1,0:T(8,128)(2,1)S(1)}, bf16[768,256]{1,0:T(8,128)(2,1)}, u32[]{:S(2)}) copy-start(bf16[768,256]{1,0:T(8,128)(2,1)} %constant.18.clone.back_ref) | copy-start | bytes 1179652
  32.0 1.0 %copy-start.2 = (bf16[768,256]{1,0:T(8,128)(2,1)S(1)}, bf16[768,256]{1,0:T(8,128)(2,1)}, u32[]{:S(2)}) copy-start(bf16[768,256]{1,0:T(8,128)(2,1)} %constant.17.clone.into_ref) | copy-start | bytes 1179652
  33.0 0.7 %copy-start.7 = (f32[16]{0:T(128)S(1)}, f32[16]{0:T(128)}, u32[]{:S(2)}) copy-start(f32[16]{0:T(128)} %noise_ref.3) | copy-start | bytes 196
  53.5 0.9 %copy-start.3 = (f32[6,2,6,256]{3,2,1,0:T(8,128)S(1)}, f32[6,2,6,256]{3,2,1,0:T(8,128)}, u32[]{:S(2)}) copy-start(f32[6,2,6,256]{3,2,1,0:T(8,128)} %constant.20.clone.turns_ref) | copy-start | bytes 221188

commit v5 on v4

--- a/solution.py
+++ b/solution.py
@@ -18,15 +18,16 @@
 BF16 = jnp.bfloat16
 SUB = 8
 LANES = 128
+PER_HOUR = 5
 STEP = 120
 STEP_BACK = 240
 MIB = 2**20
 
 
-def stacked(table):
+def halves(table):
     high = table.astype(ml_dtypes.bfloat16)
     low = (table - high.astype(np.float64)).astype(ml_dtypes.bfloat16)
-    return np.concatenate([high, high, low], axis=-2)
+    return np.concatenate([high, low], axis=-2)
 
 
 def lon_basis(size):
@@ -77,12 +78,13 @@
     slots, owners, _ = head.shape
     into = np.concatenate([head[..., :STEP].transpose(0, 2, 1), turns.reshape(slots, -1, owners)], axis=1)
     head, turns = lon_tables(lon_size, STEP_BACK, blocks, bands)
-    back = stacked(head).reshape(-1, head.shape[-1])
+    back = halves(head).reshape(-1, head.shape[-1])
     by_lat = lat_basis(lat_size).reshape(lat_size, bands, lat_size // bands)
     by_lat = by_lat.transpose(0, 2, 1).reshape(lat_size, lat_size)
     pad = -lat_size % (2 * LANES)
     by_lat = np.pad(by_lat, ((0, pad), (0, pad)))
-    return into.astype(np.float32), back, turns, stacked(by_lat.T), stacked(by_lat)
+    later = np.concatenate([halves(by_lat.T), halves(by_lat), back], axis=0)
+    return into.astype(np.float32), later, turns.reshape(-1, SUB, owners)
 
 
 def split(value):
@@ -95,8 +97,13 @@
     return jnp.concatenate([high, low, high], axis=1)
 
 
+def facing(table):
+    depth = table.shape[0] // 2
+    return [table[:depth], table[:depth], table[depth:]]
+
+
 def product(value, table):
-    return jnp.dot(spread(value), table, preferred_element_type=F32)
+    return jnp.dot(spread(value), jnp.concatenate(facing(table), axis=0), preferred_element_type=F32)
 
 
 def partners(value, bands):
@@ -138,10 +145,26 @@
     out_ref[...] = slots_of[...].T
 
 
-def gains_kernel(slots, where_ref, noise_ref, var_ref, scale_ref, out_ref, var, scale):
+def gains_kernel(
+    slots, where_ref, noise_hbm, var_hbm, scale_hbm, later_hbm, turns_hbm,
+    out_ref, later_ref, noise_ref, var_ref, scale_ref, var, scale, sems,
+):
+    pairs = (
+        (noise_hbm, noise_ref),
+        (var_hbm, var_ref),
+        (scale_hbm, scale_ref),
+        (later_hbm, later_ref),
+        (turns_hbm, out_ref.at[: turns_hbm.shape[0]]),
+    )
+    fetch = [pltpu.make_async_copy(here, there, sems.at[i]) for i, (here, there) in enumerate(pairs)]
+    for copy in fetch:
+        copy.start()
+    first_gain = turns_hbm.shape[0]
     last = var_ref.shape[0] - 1
     var[...] = jnp.ones_like(var)
     scale[...] = jnp.ones_like(scale)
+    for copy in fetch[:3]:
+        copy.wait()
     for m in range(slots):
         row = jnp.minimum(slots * where_ref[0] + m, last)
         var[m : m + 1, : var_ref.shape[1]] = var_ref[pl.ds(row, 1), :]
@@ -163,7 +186,7 @@
     ]
     for i in range(3):
         for j in range(3):
-            out_ref[3 * i + j] = a[i][j]
+            out_ref[first_gain + 3 * i + j] = a[i][j]
 
     def carried(cov):
         ap = [[a[i][0] * cov[0][j] + a[i][1] * cov[1][j] + a[i][2] * cov[2][j] for j in range(3)] for i in range(3)]
@@ -177,25 +200,29 @@
     cov = [[variance * STATIONARY[i][j] for j in range(3)] for i in range(3)]
     start = carried(cov)
     noise_cov = [[cov[i][j] - start[i][j] for j in range(3)] for i in range(3)]
-    for h in range((out_ref.shape[0] - 9) // 4):
+    for h in range((out_ref.shape[0] - first_gain - 9) // PER_HOUR):
+        at = first_gain + 9 + PER_HOUR * h
         noise = noise_ref[h]
         moved = carried(cov)
         pm = {(i, j): moved[i][j] + noise_cov[i][j] for i in range(3) for j in range(i, 3)}
         inverse = 1.0 / (pm[0, 0] + noise)
         k = [pm[0, j] * inverse for j in range(3)]
         for j in range(3):
-            out_ref[9 + 4 * h + j] = k[j]
-        out_ref[9 + 4 * h + 3] = inverse
+            out_ref[at + j] = k[j]
+        out_ref[at + 3] = inverse
+        out_ref[at + 4] = jnp.full(inverse.shape, noise, F32)
         first = [noise * k[j] for j in range(3)]
         c11 = pm[1, 1] - k[1] * pm[0, 1]
         c12 = pm[1, 2] - k[1] * pm[0, 2]
         c22 = pm[2, 2] - k[2] * pm[0, 2]
         cov = [[first[0], first[1], first[2]], [first[1], c11, c12], [first[2], c12, c22]]
-
-
-def smooth_kernel(lats, bands, noise_ref, x_ref, gain_ref, into_ref, back_ref, out_ref, turned, grid, series):
+    for copy in fetch[3:]:
+        copy.wait()
+
+
+def smooth_kernel(lats, bands, first_gain, x_ref, gain_ref, later_ref, out_ref, turned, grid, series):
     owners, lanes = x_ref.shape
-    hours = (gain_ref.shape[0] - 9) // 4
+    hours = (gain_ref.shape[0] - first_gain - 9) // PER_HOUR
     blocks = owners // bands
     per_block = hours // blocks
     stride = per_block * SUB
@@ -203,6 +230,7 @@
     for part in range(parts):
         turned[part] = x_ref[part * width : (part + 1) * width, :].T
     per_part = width // bands
+    depth = 2 * grid.shape[1]
     grid[:, lats * bands :] = jnp.zeros((grid.shape[0], grid.shape[1] - lats * bands), F32)
     for h in range(per_block):
         for lat in range(lats):
@@ -211,35 +239,36 @@
                 for t in range(per_part):
                     at = ((part * per_part + t) * per_block + h) * SUB
                     grid[at : at + SUB, lat * bands : (lat + 1) * bands] = rows[:, t * bands : (t + 1) * bands]
-    series[...] = product(grid[...], into_ref[...])
-
-    a = [[gain_ref[3 * i + j] for j in range(3)] for i in range(3)]
+    series[...] = product(grid[...], later_ref[:depth, :])
+
+    a = [[gain_ref[first_gain + 3 * i + j] for j in range(3)] for i in range(3)]
+    gain = lambda h, which: gain_ref[first_gain + 9 + PER_HOUR * h + which]
     scaled = []
     mean = None
     for h in range(hours):
         seen = series[h * SUB : (h + 1) * SUB, :]
         if mean is None:
             error = seen
-            mean = [gain_ref[9 + 4 * h + j] * error for j in range(3)]
+            mean = [gain(h, j) * error for j in range(3)]
         else:
             ahead = [a[i][0] * mean[0] + a[i][1] * mean[1] + a[i][2] * mean[2] for i in range(3)]
             error = seen - ahead[0]
-            mean = [ahead[j] + gain_ref[9 + 4 * h + j] * error for j in range(3)]
-        scaled.append(error * gain_ref[9 + 4 * h + 3])
+            mean = [ahead[j] + gain(h, j) * error for j in range(3)]
+        scaled.append(error * gain(h, 3))
     adjoint = None
     for h in reversed(range(hours)):
         drop = scaled[h]
         if adjoint is not None:
-            drop = drop + (gain_ref[9 + 4 * h + 0] * adjoint[0] + gain_ref[9 + 4 * h + 1] * adjoint[1] + gain_ref[9 + 4 * h + 2] * adjoint[2])
+            drop = drop + (gain(h, 0) * adjoint[0] + gain(h, 1) * adjoint[1] + gain(h, 2) * adjoint[2])
         here = slice(h * SUB, (h + 1) * SUB)
-        series[here, :] = series[here, :] - noise_ref[h] * drop
+        series[here, :] = series[here, :] - gain(h, 4) * drop
         if adjoint is None:
             adjoint = [-(a[0][j] * drop) for j in range(3)]
         else:
             less = adjoint[0] - drop
             adjoint = [a[0][j] * less + a[1][j] * adjoint[1] + a[2][j] * adjoint[2] for j in range(3)]
 
-    grid[...] = product(series[...], back_ref[...])
+    grid[...] = product(series[...], later_ref[depth : 2 * depth, :])
     turned[...] = jnp.zeros_like(turned)
     for h in range(per_block):
         for lat in range(lats):
@@ -256,21 +285,31 @@
         out_ref[part * width : (part + 1) * width, :] = turned[part].T
 
 
-def synthesise_kernel(bands, x_ref, table_ref, turns_ref, out_ref, turned, flat):
+def synthesise_kernel(bands, slots, x_ref, later_ref, turns_ref, out_ref, turned, flat):
     lats, hours, lon = out_ref.shape
-    slots = turns_ref.shape[0]
     steps = lon // STEP_BACK
     rows = 2 * SUB
     turned[...] = x_ref[...].T
+
+    def turn(m, which, b):
+        at = (2 * m + which) * steps + b
+        return turns_ref[at // SUB, at % SUB : at % SUB + 1, :]
+
     values = []
+    tables = []
+    depth = 2 * x_ref.shape[0]
+    first = later_ref.shape[0] - slots * depth
     for m in range(slots):
+        tables += facing(later_ref[first + m * depth : first + (m + 1) * depth, :])
         plain = turned[m * rows : (m + 1) * rows, :]
         cross = partners(plain, bands)
         turned_on = [
-            plain * turns_ref[m, 0, b : b + 1, :] + cross * turns_ref[m, 1, b : b + 1, :] for b in range(steps)
+            plain * turn(m, 0, b) + cross * turn(m, 1, b) for b in range(steps)
         ]
         values.append(spread(jnp.concatenate(turned_on, axis=0)))
-    total = jnp.dot(jnp.concatenate(values, axis=1), table_ref[...], preferred_element_type=F32)
+    total = jnp.dot(
+        jnp.concatenate(values, axis=1), jnp.concatenate(tables, axis=0), preferred_element_type=F32
+    )
     for b in range(steps):
         flat[:, b * STEP_BACK : (b + 1) * STEP_BACK] = total[b * rows : (b + 1) * rows, :STEP_BACK]
     for lat in range(lats):
@@ -281,13 +320,17 @@
     return pltpu.CompilerParams(vmem_limit_bytes=mib * MIB)
 
 
+def in_hbm(value):
+    return pltpu.with_memory_space_constraint(value, pltpu.HBM)
+
+
 def per_device(tables, observed, noise_var, spectral_var, time_scale):
-    lon_into, lon_back, turns, lat_into, lat_back = tables
+    lon_into, later, turns = tables
     hours_dev, lat_dev, lon_size = observed.shape
     hours = noise_var.shape[0]
     bands = lax.axis_size("space")
     slots, _, owners = lon_into.shape
-    lat_pad = lat_into.shape[-1]
+    lat_pad = later.shape[-1]
     rows = 2 * SUB
     lanes = SUB * rows
     vmem = pl.BlockSpec(memory_space=pltpu.VMEM)
@@ -310,25 +353,35 @@
         ],
         compiler_params=params(16),
         name="analyse",
-    )(*(pltpu.with_memory_space_constraint(each, pltpu.HBM) for each in (by_lat, lon_into)))
+    )(in_hbm(by_lat), in_hbm(lon_into))
     got = lax.all_to_all(sent, ("tm", "space"), split_axis=0, concat_axis=0, tiled=True)
 
     where = lax.axis_index("tm").astype(jnp.int32).reshape(1)
-    gains = pl.pallas_call(
+    gains, later = pl.pallas_call(
         functools.partial(gains_kernel, slots),
-        out_shape=jax.ShapeDtypeStruct((9 + 4 * hours, SUB, lat_pad), F32),
-        in_specs=[smem, smem, vmem, vmem],
-        out_specs=vmem,
-        scratch_shapes=[pltpu.VMEM((SUB, lat_pad), F32)] * 2,
-        cost_estimate=pl.CostEstimate(flops=200 * hours * SUB * 256, bytes_accessed=2 * MIB, transcendentals=0),
-        compiler_params=params(8),
+        out_shape=(
+            jax.ShapeDtypeStruct((turns.shape[0] + 9 + PER_HOUR * hours, SUB, lat_pad), F32),
+            jax.ShapeDtypeStruct(later.shape, BF16),
+        ),
+        in_specs=[smem] + [hbm] * 5,
+        out_specs=(vmem,) * 2,
+        scratch_shapes=[
+            pltpu.SMEM(noise_var.shape, F32),
+            pltpu.VMEM(spectral_var.shape, F32),
+            pltpu.VMEM(spectral_var.shape, F32),
+            pltpu.VMEM((SUB, lat_pad), F32),
+            pltpu.VMEM((SUB, lat_pad), F32),
+            pltpu.SemaphoreType.DMA((5,)),
+        ],
+        cost_estimate=pl.CostEstimate(flops=200 * hours * SUB * 256, bytes_accessed=8 * MIB, transcendentals=0),
+        compiler_params=params(16),
         name="gains",
-    )(where, noise_var, spectral_var, time_scale)
+    )(where, *(in_hbm(each) for each in (noise_var, spectral_var, time_scale, later, turns)))
 
     smooth = pl.pallas_call(
-        functools.partial(smooth_kernel, lat_dev, bands),
+        functools.partial(smooth_kernel, lat_dev, bands, turns.shape[0]),
         out_shape=jax.ShapeDtypeStruct((owners, lanes), F32),
-        in_specs=[smem] + [vmem] * 4,
+        in_specs=[vmem] * 3,
         out_specs=vmem,
         scratch_shapes=[
             pltpu.VMEM((owners // LANES, lanes, LANES), F32),
@@ -337,18 +390,18 @@
         ],
         compiler_params=params(16),
         name="smooth",
-    )(noise_var, got, gains, lat_into, lat_back)
+    )(got, gains, later)
     back = lax.all_to_all(smooth, ("tm", "space"), split_axis=0, concat_axis=0, tiled=True)
 
     field = pl.pallas_call(
-        functools.partial(synthesise_kernel, bands),
+        functools.partial(synthesise_kernel, bands, slots),
         out_shape=jax.ShapeDtypeStruct(by_lat.shape, F32),
         in_specs=[vmem] * 3,
         out_specs=vmem,
         scratch_shapes=[pltpu.VMEM((lanes, owners), F32), pltpu.VMEM((rows, lon_size), F32)],
         compiler_params=params(16),
         name="synthesise",
-    )(back, lon_back, turns)
+    )(back, later, gains)
     return field.transpose(1, 0, 2)
 
 

time: 56.2 us -> 51.7 us (0.920)
  local copies, waits for them, and re-layouts: 5.79 us -> 0 us
  waiting for transfers between devices: 9.38 us -> 10.9 us
    unnamed x16 -> x0, local copies, waits for them, and re-layouts: 5.79 us -> none
    all_to_all x1, waiting for transfers between devices: 9.38 us -> 10.9 us  [per_device(): lax.all_to_all(sent, ('tm', 'space'), split_axis=0, concat_axis=0, tiled=...]
  transfers between devices with their start and end apart: 1 -> 1, of which waited for: 1 -> 1; matrix products, arithmetic and copies ran while one was open for 0% -> 0% of each run, Pallas kernels for 2% -> 3%
where the time goes in v5:
time: 51.7 us; the launch traced here: 51.5 us
  blocking collectives  18.2 us (35%)
  starting transfers between devices  15.7 us (30%)
  waiting for transfers between devices  10.9 us (21%)
  Pallas kernels  6.64 us (13%)
    all_to_all x1, blocking collectives, per_device(): lax.all_to_all(smooth, ('tm', 'space'), split_axis=0, concat_axis=0, tile...  18.2 us
    all_to_all x1, starting transfers between devices, per_device(): lax.all_to_all(sent, ('tm', 'space'), split_axis=0, concat_axis=0, tiled=...  15.7 us
    all_to_all x1, waiting for transfers between devices, per_device(): lax.all_to_all(sent, ('tm', 'space'), split_axis=0, concat_axis=0, tiled=...  10.9 us
    pallas_call x1, Pallas kernels, per_device(): pl.pallas_call(functools.partial(analyse_kernel, bands), out_shape=jax.Sh...  2.51 us
    pallas_call x1, Pallas kernels, per_device(): pl.pallas_call(functools.partial(gains_kernel, slots), out_shape=(jax.Sha...  1.7 us
    pallas_call x1, Pallas kernels, per_device(): pl.pallas_call(functools.partial(synthesise_kernel, bands, slots), out_sh...  1.33 us
    pallas_call x1, Pallas kernels, per_device(): pl.pallas_call(functools.partial(smooth_kernel, lat_dev, bands, turns.sha...  1.1 us
  transfers between devices with their start and end apart: 1, of which 1 were waited for; matrix products, arithmetic and copies ran while one was open for 0% of the time, Pallas kernels for 3%

profile of v5, /device:TPU:1, one launch (start us, length us, event | category | flops | bytes accessed | tf_op | source)
XLA Modules:
  0.0 51.5 jit_solution(14783710223722243636)
XLA Ops:
  0.0 2.5 %analyse.1 = f32[256,128]{1,0:T(8,128)} custom-call(f32[6,2,1440]{2,1,0:T(2,128)} %bitcast.14, f32[6,144,256]{2,1,0:T(8,128)} %constant.12.clone.table_hbm), custom_call_target="tpu_custom_call" | custom-call | tf_op jit(solution)/shard_map/analyse/pallas_call | solution.py:341
  2.5 15.7 %all-to-all-start = ((f32[256,1,128]{2,1,0:T(1,128)}), f32[256,1,128]{2,1,0:T(1,128)S(1)}, u32[]{:S(2)}, u32[]{:S(2)}) async-start(f32[256,1,128]{2,1,0:T(1,128)} %bitcast.2), calls=%async_computation | async-start | bytes 262144 | tf_op jit(solution)/shard_map/all_to_all | solution.py:357
  18.2 1.7 %gains.1 = (f32[98,8,256]{2,1,0:T(8,128)S(1)}, bf16[4096,256]{1,0:T(8,128)(2,1)S(1)}) custom-call(s32[1]{0:T(128)} %bitcast.4.where_ref, f32[16]{0:T(128)} %noise_hbm.1, f32[45,192]{1,0:T(8,128)} %var_hbm.1, f32[45,192]{1,0:T(8,128)} %scale_hbm.1, bf16[4096,256]{1,0:T(8,128)(2,1)} %constant.13.clone.later_hbm, f32[9,8,256]{2,1,0:T(8,128)} %constant.14.clone.turns_hbm), custom_call_target="tpu_custom_call" | custom-call | flops 6553600 | bytes 8388608 | tf_op jit(solution)/shard_map/gains/pallas_call | solution.py:360
  19.9 10.9 %all-to-all-done = f32[256,1,128]{2,1,0:T(1,128)S(1)} async-done(((f32[256,1,128]{2,1,0:T(1,128)}), f32[256,1,128]{2,1,0:T(1,128)S(1)}, u32[]{:S(2)}, u32[]{:S(2)}) %all-to-all-start) | async-done | bytes 131104 | tf_op jit(solution)/shard_map/all_to_all | solution.py:357
  30.8 1.1 %smooth.1 = f32[256,128]{1,0:T(8,128)S(1)} custom-call(f32[256,128]{1,0:T(8,128)S(1)} %bitcast.11, f32[98,8,256]{2,1,0:T(8,128)S(1)} %get-tuple-element.7.gain_ref.turns_ref, bf16[4096,256]{1,0:T(8,128)(2,1)S(1)} %get-tuple-element.8.later_ref), custom_call_target="tpu_custom_call" | custom-call | tf_op jit(solution)/shard_map/smooth/pallas_call | solution.py:381
  31.9 18.2 %all_to_all.22 = f32[256,1,128]{2,1,0:T(1,128)S(1)} all-to-all(f32[256,1,128]{2,1,0:T(1,128)S(1)} %bitcast.13), channel_id=1, replica_groups=mesh['tm'=8,'space'=32] {'tm','space'}, dimensions={0} | all-to-all | bytes 262144 | tf_op jit(solution)/shard_map/all_to_all | solution.py:394
  50.2 1.3 %synthesise.1 = f32[6,2,1440]{2,1,0:T(2,128)} custom-call(f32[256,128]{1,0:T(8,128)S(1)} %bitcast.12, bf16[4096,256]{1,0:T(8,128)(2,1)S(1)} %get-tuple-element.8.later_ref, f32[98,8,256]{2,1,0:T(8,128)S(1)} %get-tuple-element.7.gain_ref.turns_ref), custom_call_target="tpu_custom_call" | custom-call | tf_op jit(solution)/shard_map/synthesise/pallas_call | solution.py:396
Async XLA Ops:
  2.5 28.3 %all-to-all-start = ((f32[256,1,128]{2,1,0:T(1,128)}), f32[256,1,128]{2,1,0:T(1,128)S(1)}, u32[]{:S(2)}, u32[]{:S(2)}) async-start(f32[256,1,128]{2,1,0:T(1,128)} %bitcast.2), calls=%async_computation | async-start | bytes 262144 | tf_op jit(solution)/shard_map/all_to_all | solution.py:357

commit v6 on v5

--- a/solution.py
+++ b/solution.py
@@ -113,60 +113,12 @@
     return jnp.where(upper, pltpu.roll(value, half, 1), pltpu.roll(value, width - half, 1))
 
 
-def analyse_kernel(bands, x_hbm, table_hbm, out_ref, x, table, flat, blocks, slots_of, sems):
-    lats, hours, lon = x.shape
-    slots = table.shape[0]
-    steps = lon // STEP
-    rows = 2 * SUB
-    fetch = [pltpu.make_async_copy(x_hbm, x, sems.at[0]), pltpu.make_async_copy(table_hbm, table, sems.at[1])]
-    for copy in fetch:
-        copy.start()
-    flat[...] = jnp.zeros_like(flat)
-    blocks[...] = jnp.zeros_like(blocks)
-    slots_of[...] = jnp.zeros_like(slots_of)
-    fetch[0].wait()
-    for lat in range(lats):
-        flat[lat * hours : (lat + 1) * hours, :] = x[lat]
-    for b in range(steps):
-        blocks[b * rows : (b + 1) * rows, :STEP] = flat[:, b * STEP : (b + 1) * STEP]
-    value = spread(blocks[...])
-    fetch[1].wait()
-    for m in range(slots):
-        high, low = split(table[m, :LANES, :])
-        part = jnp.dot(value, jnp.concatenate([high, high, low], axis=0), preferred_element_type=F32)
-        straight = crossed = None
-        for b in range(steps):
-            here = part[b * rows : (b + 1) * rows]
-            plain = here * table[m, STEP + b : STEP + b + 1, :]
-            cross = here * table[m, STEP + steps + b : STEP + steps + b + 1, :]
-            straight = plain if straight is None else straight + plain
-            crossed = cross if crossed is None else crossed + cross
-        slots_of[m * rows : (m + 1) * rows, :] = straight + partners(crossed, bands)
-    out_ref[...] = slots_of[...].T
-
-
-def gains_kernel(
-    slots, where_ref, noise_hbm, var_hbm, scale_hbm, later_hbm, turns_hbm,
-    out_ref, later_ref, noise_ref, var_ref, scale_ref, var, scale, sems,
-):
-    pairs = (
-        (noise_hbm, noise_ref),
-        (var_hbm, var_ref),
-        (scale_hbm, scale_ref),
-        (later_hbm, later_ref),
-        (turns_hbm, out_ref.at[: turns_hbm.shape[0]]),
-    )
-    fetch = [pltpu.make_async_copy(here, there, sems.at[i]) for i, (here, there) in enumerate(pairs)]
-    for copy in fetch:
-        copy.start()
-    first_gain = turns_hbm.shape[0]
+def fill_gains(slots, first_gain, out_ref, noise_ref, var_ref, scale_ref, var, scale):
     last = var_ref.shape[0] - 1
     var[...] = jnp.ones_like(var)
     scale[...] = jnp.ones_like(scale)
-    for copy in fetch[:3]:
-        copy.wait()
     for m in range(slots):
-        row = jnp.minimum(slots * where_ref[0] + m, last)
+        row = jnp.minimum(slots * lax.axis_index("tm") + m, last)
         var[m : m + 1, : var_ref.shape[1]] = var_ref[pl.ds(row, 1), :]
         scale[m : m + 1, : var_ref.shape[1]] = scale_ref[pl.ds(row, 1), :]
     variance = var[...]
@@ -216,7 +168,53 @@
         c12 = pm[1, 2] - k[1] * pm[0, 2]
         c22 = pm[2, 2] - k[2] * pm[0, 2]
         cov = [[first[0], first[1], first[2]], [first[1], c11, c12], [first[2], c12, c22]]
-    for copy in fetch[3:]:
+
+
+def analyse_kernel(
+    bands, x_hbm, table_hbm, noise_hbm, var_hbm, scale_hbm, turns_hbm, later_hbm, out_ref, gain_ref,
+    later_ref, x, table, flat, blocks, slots_of, noise_ref, var_ref, scale_ref, var, scale, sems,
+):
+    lats, hours, lon = x.shape
+    slots = table.shape[0]
+    steps = lon // STEP
+    rows = 2 * SUB
+    pairs = (
+        (x_hbm, x),
+        (table_hbm, table),
+        (noise_hbm, noise_ref),
+        (var_hbm, var_ref),
+        (scale_hbm, scale_ref),
+        (turns_hbm, gain_ref.at[: turns_hbm.shape[0]]),
+        (later_hbm, later_ref),
+    )
+    fetch = [pltpu.make_async_copy(here, there, sems.at[i]) for i, (here, there) in enumerate(pairs)]
+    for copy in fetch:
+        copy.start()
+    flat[...] = jnp.zeros_like(flat)
+    blocks[...] = jnp.zeros_like(blocks)
+    slots_of[...] = jnp.zeros_like(slots_of)
+    fetch[0].wait()
+    for lat in range(lats):
+        flat[lat * hours : (lat + 1) * hours, :] = x[lat]
+    for b in range(steps):
+        blocks[b * rows : (b + 1) * rows, :STEP] = flat[:, b * STEP : (b + 1) * STEP]
+    value = spread(blocks[...])
+    for copy in fetch[1:5]:
+        copy.wait()
+    fill_gains(slots, turns_hbm.shape[0], gain_ref, noise_ref, var_ref, scale_ref, var, scale)
+    for m in range(slots):
+        high, low = split(table[m, :LANES, :])
+        part = jnp.dot(value, jnp.concatenate([high, high, low], axis=0), preferred_element_type=F32)
+        straight = crossed = None
+        for b in range(steps):
+            here = part[b * rows : (b + 1) * rows]
+            plain = here * table[m, STEP + b : STEP + b + 1, :]
+            cross = here * table[m, STEP + steps + b : STEP + steps + b + 1, :]
+            straight = plain if straight is None else straight + plain
+            crossed = cross if crossed is None else crossed + cross
+        slots_of[m * rows : (m + 1) * rows, :] = straight + partners(crossed, bands)
+    out_ref[...] = slots_of[...].T
+    for copy in fetch[5:]:
         copy.wait()
 
 
@@ -338,45 +336,32 @@
     hbm = pl.BlockSpec(memory_space=pltpu.HBM)
 
     by_lat = observed.transpose(1, 0, 2)
-    sent = pl.pallas_call(
+    sent, gains, later = pl.pallas_call(
         functools.partial(analyse_kernel, bands),
-        out_shape=jax.ShapeDtypeStruct((owners, lanes), F32),
-        in_specs=[hbm] * 2,
-        out_specs=vmem,
+        out_shape=(
+            jax.ShapeDtypeStruct((owners, lanes), F32),
+            jax.ShapeDtypeStruct((turns.shape[0] + 9 + PER_HOUR * hours, SUB, lat_pad), F32),
+            jax.ShapeDtypeStruct(later.shape, BF16),
+        ),
+        in_specs=[hbm] * 7,
+        out_specs=(vmem,) * 3,
         scratch_shapes=[
             pltpu.VMEM(by_lat.shape, F32),
             pltpu.VMEM(lon_into.shape, F32),
             pltpu.VMEM((rows, lon_size), F32),
             pltpu.VMEM((lon_size // STEP * rows, LANES), F32),
             pltpu.VMEM((lanes, owners), F32),
-            pltpu.SemaphoreType.DMA((2,)),
-        ],
-        compiler_params=params(16),
-        name="analyse",
-    )(in_hbm(by_lat), in_hbm(lon_into))
-    got = lax.all_to_all(sent, ("tm", "space"), split_axis=0, concat_axis=0, tiled=True)
-
-    where = lax.axis_index("tm").astype(jnp.int32).reshape(1)
-    gains, later = pl.pallas_call(
-        functools.partial(gains_kernel, slots),
-        out_shape=(
-            jax.ShapeDtypeStruct((turns.shape[0] + 9 + PER_HOUR * hours, SUB, lat_pad), F32),
-            jax.ShapeDtypeStruct(later.shape, BF16),
-        ),
-        in_specs=[smem] + [hbm] * 5,
-        out_specs=(vmem,) * 2,
-        scratch_shapes=[
             pltpu.SMEM(noise_var.shape, F32),
             pltpu.VMEM(spectral_var.shape, F32),
             pltpu.VMEM(spectral_var.shape, F32),
             pltpu.VMEM((SUB, lat_pad), F32),
             pltpu.VMEM((SUB, lat_pad), F32),
-            pltpu.SemaphoreType.DMA((5,)),
+            pltpu.SemaphoreType.DMA((7,)),
         ],
-        cost_estimate=pl.CostEstimate(flops=200 * hours * SUB * 256, bytes_accessed=8 * MIB, transcendentals=0),
         compiler_params=params(16),
-        name="gains",
-    )(where, *(in_hbm(each) for each in (noise_var, spectral_var, time_scale, later, turns)))
+        name="analyse",
+    )(*(in_hbm(each) for each in (by_lat, lon_into, noise_var, spectral_var, time_scale, turns, later)))
+    got = lax.all_to_all(sent, ("tm", "space"), split_axis=0, concat_axis=0, tiled=True)
 
     smooth = pl.pallas_call(
         functools.partial(smooth_kernel, lat_dev, bands, turns.shape[0]),

time: 51.7 us -> 51.2 us (level)
  blocking collectives: 18.2 us -> 46.4 us
  starting transfers between devices: 15.7 us -> 0 us
  waiting for transfers between devices: 10.9 us -> 0 us
  Pallas kernels: 6.64 us -> 4.7 us
    all_to_all x0 -> x1, blocking collectives: none -> 28.1 us  [per_device(): lax.all_to_all(sent, ('tm', 'space'), split_axis=0, concat_axis=0, tiled=...]
    all_to_all x1 -> x0, starting transfers between devices: 15.7 us -> none  [per_device(): lax.all_to_all(sent, ('tm', 'space'), split_axis=0, concat_axis=0, tiled=...]
    all_to_all x1 -> x0, waiting for transfers between devices: 10.9 us -> none  [per_device(): lax.all_to_all(sent, ('tm', 'space'), split_axis=0, concat_axis=0, tiled=...]
    pallas_call x2 -> x1, Pallas kernels: 4.22 us -> 2.28 us  [per_device(): pl.pallas_call(functools.partial(analyse_kernel, bands), out_shape=(jax.S...]
  transfers between devices with their start and end apart: 1 -> 0, of which waited for: 1 -> 0; matrix products, arithmetic and copies ran while one was open for 0% -> 0% of each run, Pallas kernels for 3% -> 0%
where the time goes in v6:
time: 51.2 us; the launch traced here: 51.1 us
  blocking collectives  46.4 us (91%)
  Pallas kernels  4.7 us (9%)
    all_to_all x1, blocking collectives, per_device(): lax.all_to_all(sent, ('tm', 'space'), split_axis=0, concat_axis=0, tiled=...  28.1 us
    all_to_all x1, blocking collectives, per_device(): lax.all_to_all(smooth, ('tm', 'space'), split_axis=0, concat_axis=0, tile...  18.2 us
    pallas_call x1, Pallas kernels, per_device(): pl.pallas_call(functools.partial(analyse_kernel, bands), out_shape=(jax.S...  2.28 us
    pallas_call x1, Pallas kernels, per_device(): pl.pallas_call(functools.partial(synthesise_kernel, bands, slots), out_sh...  1.33 us
    pallas_call x1, Pallas kernels, per_device(): pl.pallas_call(functools.partial(smooth_kernel, lat_dev, bands, turns.sha...  1.1 us

profile of v6, /device:TPU:1, one launch (start us, length us, event | category | flops | bytes accessed | tf_op | source)
XLA Modules:
  0.0 51.1 jit_solution(14621797077307084440)
XLA Ops:
  0.0 2.3 %analyse.1 = (f32[256,128]{1,0:T(8,128)S(1)}, f32[98,8,256]{2,1,0:T(8,128)S(1)}, bf16[4096,256]{1,0:T(8,128)(2,1)S(1)}) custom-call(f32[6,2,1440]{2,1,0:T(2,128)} %bitcast.14, f32[6,144,256]{2,1,0:T(8,128)} %constant.6.clone.table_hbm, f32[16]{0:T(128)} %noise_hbm.1, f32[45,192]{1,0:T(8,128)} %var_hbm.1, f32[45,192]{1,0:T(8,128)} %scale_hbm.1, ...), custom_call_target="tpu_custom_call" | custom-call | tf_op jit(solution)/shard_map/analyse/pallas_call | solution.py:339
  2.3 28.1 %all_to_all.22 = f32[256,1,128]{2,1,0:T(1,128)S(1)} all-to-all(f32[256,1,128]{2,1,0:T(1,128)S(1)} %bitcast.13), channel_id=1, replica_groups=mesh['tm'=8,'space'=32] {'tm','space'}, dimensions={0} | all-to-all | bytes 262144 | tf_op jit(solution)/shard_map/all_to_all | solution.py:364
  30.4 1.1 %smooth.1 = f32[256,128]{1,0:T(8,128)S(1)} custom-call(f32[256,128]{1,0:T(8,128)S(1)} %bitcast.11, f32[98,8,256]{2,1,0:T(8,128)S(1)} %get-tuple-element.9.gain_ref.turns_ref, bf16[4096,256]{1,0:T(8,128)(2,1)S(1)} %get-tuple-element.10.later_ref), custom_call_target="tpu_custom_call" | custom-call | tf_op jit(solution)/shard_map/smooth/pallas_call | solution.py:366
  31.5 18.2 %all_to_all.23 = f32[256,1,128]{2,1,0:T(1,128)S(1)} all-to-all(f32[256,1,128]{2,1,0:T(1,128)S(1)} %bitcast.12), channel_id=1, replica_groups=mesh['tm'=8,'space'=32] {'tm','space'}, dimensions={0} | all-to-all | bytes 262144 | tf_op jit(solution)/shard_map/all_to_all | solution.py:379
  49.7 1.3 %synthesise.1 = f32[6,2,1440]{2,1,0:T(2,128)} custom-call(f32[256,128]{1,0:T(8,128)S(1)} %bitcast.10, bf16[4096,256]{1,0:T(8,128)(2,1)S(1)} %get-tuple-element.10.later_ref, f32[98,8,256]{2,1,0:T(8,128)S(1)} %get-tuple-element.9.gain_ref.turns_ref), custom_call_target="tpu_custom_call" | custom-call | tf_op jit(solution)/shard_map/synthesise/pallas_call | solution.py:381

commit v7 on v6

--- a/solution.py
+++ b/solution.py
@@ -95,6 +95,12 @@
 def spread(value):
     high, low = split(value)
     return jnp.concatenate([high, low, high], axis=1)
+
+
+def folded_product(high, low, table_high, table_low):
+    rows = high.shape[0]
+    both = jnp.dot(jnp.concatenate([high, low], axis=0), table_high, preferred_element_type=F32)
+    return both[:rows] + both[rows:] + jnp.dot(high, table_low, preferred_element_type=F32)
 
 
 def facing(table):
@@ -179,11 +185,11 @@
     steps = lon // STEP
     rows = 2 * SUB
     pairs = (
+        (var_hbm, var_ref),
+        (scale_hbm, scale_ref),
+        (noise_hbm, noise_ref),
         (x_hbm, x),
         (table_hbm, table),
-        (noise_hbm, noise_ref),
-        (var_hbm, var_ref),
-        (scale_hbm, scale_ref),
         (turns_hbm, gain_ref.at[: turns_hbm.shape[0]]),
         (later_hbm, later_ref),
     )
@@ -193,15 +199,16 @@
     flat[...] = jnp.zeros_like(flat)
     blocks[...] = jnp.zeros_like(blocks)
     slots_of[...] = jnp.zeros_like(slots_of)
-    fetch[0].wait()
+    for copy in fetch[:3]:
+        copy.wait()
+    fill_gains(slots, turns_hbm.shape[0], gain_ref, noise_ref, var_ref, scale_ref, var, scale)
+    fetch[3].wait()
     for lat in range(lats):
         flat[lat * hours : (lat + 1) * hours, :] = x[lat]
     for b in range(steps):
         blocks[b * rows : (b + 1) * rows, :STEP] = flat[:, b * STEP : (b + 1) * STEP]
     value = spread(blocks[...])
-    for copy in fetch[1:5]:
-        copy.wait()
-    fill_gains(slots, turns_hbm.shape[0], gain_ref, noise_ref, var_ref, scale_ref, var, scale)
+    fetch[4].wait()
     for m in range(slots):
         high, low = split(table[m, :LANES, :])
         part = jnp.dot(value, jnp.concatenate([high, high, low], axis=0), preferred_element_type=F32)
@@ -294,20 +301,23 @@
         return turns_ref[at // SUB, at % SUB : at % SUB + 1, :]
 
     values = []
-    tables = []
+    highs = []
+    lows = []
     depth = 2 * x_ref.shape[0]
     first = later_ref.shape[0] - slots * depth
     for m in range(slots):
-        tables += facing(later_ref[first + m * depth : first + (m + 1) * depth, :])
+        at = first + m * depth
+        highs.append(later_ref[at : at + depth // 2, :])
+        lows.append(later_ref[at + depth // 2 : at + depth, :])
         plain = turned[m * rows : (m + 1) * rows, :]
         cross = partners(plain, bands)
         turned_on = [
             plain * turn(m, 0, b) + cross * turn(m, 1, b) for b in range(steps)
         ]
-        values.append(spread(jnp.concatenate(turned_on, axis=0)))
-    total = jnp.dot(
-        jnp.concatenate(values, axis=1), jnp.concatenate(tables, axis=0), preferred_element_type=F32
-    )
+        values.append(split(jnp.concatenate(turned_on, axis=0)))
+    high = jnp.concatenate([each[0] for each in values], axis=1)
+    low = jnp.concatenate([each[1] for each in values], axis=1)
+    total = folded_product(high, low, jnp.concatenate(highs, axis=0), jnp.concatenate(lows, axis=0))
     for b in range(steps):
         flat[:, b * STEP_BACK : (b + 1) * STEP_BACK] = total[b * rows : (b + 1) * rows, :STEP_BACK]
     for lat in range(lats):

time: 51.2 us -> 51 us (level)
  no operation moved by 1% of the time
where the time goes in v7:
time: 51 us; the launch traced here: 50.9 us
  blocking collectives  46.4 us (91%)
  Pallas kernels  4.5 us (9%)
    all_to_all x1, blocking collectives, per_device(): lax.all_to_all(sent, ('tm', 'space'), split_axis=0, concat_axis=0, tiled=...  28.1 us
    all_to_all x1, blocking collectives, per_device(): lax.all_to_all(smooth, ('tm', 'space'), split_axis=0, concat_axis=0, tile...  18.2 us
    pallas_call x1, Pallas kernels, per_device(): pl.pallas_call(functools.partial(analyse_kernel, bands), out_shape=(jax.S...  2.15 us
    pallas_call x1, Pallas kernels, per_device(): pl.pallas_call(functools.partial(synthesise_kernel, bands, slots), out_sh...  1.26 us
    pallas_call x1, Pallas kernels, per_device(): pl.pallas_call(functools.partial(smooth_kernel, lat_dev, bands, turns.sha...  1.09 us

profile of v7, /device:TPU:1, one launch (start us, length us, event | category | flops | bytes accessed | tf_op | source)
XLA Modules:
  0.0 50.9 jit_solution(8298437044014518128)
XLA Ops:
  0.0 2.1 %analyse.1 = (f32[256,128]{1,0:T(8,128)S(1)}, f32[98,8,256]{2,1,0:T(8,128)S(1)}, bf16[4096,256]{1,0:T(8,128)(2,1)S(1)}) custom-call(f32[6,2,1440]{2,1,0:T(2,128)} %bitcast.14, f32[6,144,256]{2,1,0:T(8,128)} %constant.6.clone.table_hbm, f32[16]{0:T(128)} %noise_hbm.1, f32[45,192]{1,0:T(8,128)} %var_hbm.1, f32[45,192]{1,0:T(8,128)} %scale_hbm.1, ...), custom_call_target="tpu_custom_call" | custom-call | tf_op jit(solution)/shard_map/analyse/pallas_call | solution.py:349
  2.2 28.1 %all_to_all.22 = f32[256,1,128]{2,1,0:T(1,128)S(1)} all-to-all(f32[256,1,128]{2,1,0:T(1,128)S(1)} %bitcast.13), channel_id=1, replica_groups=mesh['tm'=8,'space'=32] {'tm','space'}, dimensions={0} | all-to-all | bytes 262144 | tf_op jit(solution)/shard_map/all_to_all | solution.py:374
  30.3 1.1 %smooth.1 = f32[256,128]{1,0:T(8,128)S(1)} custom-call(f32[256,128]{1,0:T(8,128)S(1)} %bitcast.11, f32[98,8,256]{2,1,0:T(8,128)S(1)} %get-tuple-element.9.gain_ref.turns_ref, bf16[4096,256]{1,0:T(8,128)(2,1)S(1)} %get-tuple-element.10.later_ref), custom_call_target="tpu_custom_call" | custom-call | tf_op jit(solution)/shard_map/smooth/pallas_call | solution.py:376
  31.4 18.2 %all_to_all.23 = f32[256,1,128]{2,1,0:T(1,128)S(1)} all-to-all(f32[256,1,128]{2,1,0:T(1,128)S(1)} %bitcast.12), channel_id=1, replica_groups=mesh['tm'=8,'space'=32] {'tm','space'}, dimensions={0} | all-to-all | bytes 262144 | tf_op jit(solution)/shard_map/all_to_all | solution.py:389
  49.6 1.3 %synthesise.1 = f32[6,2,1440]{2,1,0:T(2,128)} custom-call(f32[256,128]{1,0:T(8,128)S(1)} %bitcast.10, bf16[4096,256]{1,0:T(8,128)(2,1)S(1)} %get-tuple-element.10.later_ref, f32[98,8,256]{2,1,0:T(8,128)S(1)} %get-tuple-element.9.gain_ref.turns_ref), custom_call_target="tpu_custom_call" | custom-call | tf_op jit(solution)/shard_map/synthesise/pallas_call | solution.py:391

commit v8 on v7

--- a/solution.py
+++ b/solution.py
@@ -11,9 +11,8 @@
 from jax.sharding import PartitionSpec as P
 
 ROOT_FIVE = 2.23606797749979
-NILPOTENT = ((1.0, 1.0, 0.0), (0.0, 1.0, 1.0), (-1.0, -3.0, -2.0))
-NILPOTENT_SQUARED = ((1.0, 2.0, 1.0), (-1.0, -2.0, -1.0), (1.0, 2.0, 1.0))
-STATIONARY = ((1.0, 0.0, -1.0 / 3.0), (0.0, 1.0 / 3.0, 0.0), (-1.0 / 3.0, 0.0, 1.0))
+STATIONARY = ((1.0, 1.0, 2.0 / 3.0), (1.0, 4.0 / 3.0, 4.0 / 3.0), (2.0 / 3.0, 4.0 / 3.0, 8.0 / 3.0))
+MOVES = 3
 F32 = jnp.float32
 BF16 = jnp.bfloat16
 SUB = 8
@@ -130,50 +129,47 @@
     variance = var[...]
     rate = ROOT_FIVE / scale[...]
     damping = jnp.exp(-rate)
-    a = [
-        [
-            damping
-            * (
-                (1.0 if i == j else 0.0)
-                + rate * NILPOTENT[i][j]
-                + 0.5 * rate * rate * NILPOTENT_SQUARED[i][j]
-            )
-            for j in range(3)
-        ]
-        for i in range(3)
-    ]
-    for i in range(3):
-        for j in range(3):
-            out_ref[first_gain + 3 * i + j] = a[i][j]
-
-    def carried(cov):
-        ap = [[a[i][0] * cov[0][j] + a[i][1] * cov[1][j] + a[i][2] * cov[2][j] for j in range(3)] for i in range(3)]
-        upper = {
-            (i, j): ap[i][0] * a[j][0] + ap[i][1] * a[j][1] + ap[i][2] * a[j][2]
-            for i in range(3)
-            for j in range(i, 3)
+    half_square = 0.5 * rate * rate
+    for i, move in enumerate((damping, damping * rate, damping * half_square)):
+        out_ref[first_gain + i] = move
+    twice = damping * damping
+
+    def carried(p):
+        top = [p[0, j] + rate * p[1, j] + half_square * p[2, j] for j in range(3)]
+        middle = [p[1, j] + rate * p[2, j] for j in range(3)]
+        full = {
+            (0, 0): top[0] + rate * top[1] + half_square * top[2],
+            (0, 1): top[1] + rate * top[2],
+            (0, 2): top[2],
+            (1, 1): middle[1] + rate * middle[2],
+            (1, 2): middle[2],
+            (2, 2): p[2, 2],
         }
-        return [[upper[min(i, j), max(i, j)] for j in range(3)] for i in range(3)]
-
-    cov = [[variance * STATIONARY[i][j] for j in range(3)] for i in range(3)]
-    start = carried(cov)
-    noise_cov = [[cov[i][j] - start[i][j] for j in range(3)] for i in range(3)]
-    for h in range((out_ref.shape[0] - first_gain - 9) // PER_HOUR):
-        at = first_gain + 9 + PER_HOUR * h
+        return {at: twice * each for at, each in full.items()}
+
+    def symmetric(upper):
+        return {(i, j): upper[min(i, j), max(i, j)] for i in range(3) for j in range(3)}
+
+    start = {(i, j): variance * STATIONARY[i][j] for i in range(3) for j in range(i, 3)}
+    moved = carried(symmetric(start))
+    noise_cov = {at: start[at] - moved[at] for at in start}
+    pm = start
+    for h in range((out_ref.shape[0] - first_gain - MOVES) // PER_HOUR):
+        at = first_gain + MOVES + PER_HOUR * h
         noise = noise_ref[h]
-        moved = carried(cov)
-        pm = {(i, j): moved[i][j] + noise_cov[i][j] for i in range(3) for j in range(i, 3)}
+        if h > 0:
+            moved = carried(symmetric(cov))
+            pm = {entry: moved[entry] + noise_cov[entry] for entry in moved}
         inverse = 1.0 / (pm[0, 0] + noise)
         k = [pm[0, j] * inverse for j in range(3)]
         for j in range(3):
             out_ref[at + j] = k[j]
         out_ref[at + 3] = inverse
         out_ref[at + 4] = jnp.full(inverse.shape, noise, F32)
-        first = [noise * k[j] for j in range(3)]
-        c11 = pm[1, 1] - k[1] * pm[0, 1]
-        c12 = pm[1, 2] - k[1] * pm[0, 2]
-        c22 = pm[2, 2] - k[2] * pm[0, 2]
-        cov = [[first[0], first[1], first[2]], [first[1], c11, c12], [first[2], c12, c22]]
+        cov = {(0, j): noise * k[j] for j in range(3)}
+        for i in (1, 2):
+            for j in range(i, 3):
+                cov[i, j] = pm[i, j] - k[i] * pm[0, j]
 
 
 def analyse_kernel(
@@ -227,7 +223,7 @@
 
 def smooth_kernel(lats, bands, first_gain, x_ref, gain_ref, later_ref, out_ref, turned, grid, series):
     owners, lanes = x_ref.shape
-    hours = (gain_ref.shape[0] - first_gain - 9) // PER_HOUR
+    hours = (gain_ref.shape[0] - first_gain - MOVES) // PER_HOUR
     blocks = owners // bands
     per_block = hours // blocks
     stride = per_block * SUB
@@ -246,8 +242,8 @@
                     grid[at : at + SUB, lat * bands : (lat + 1) * bands] = rows[:, t * bands : (t + 1) * bands]
     series[...] = product(grid[...], later_ref[:depth, :])
 
-    a = [[gain_ref[first_gain + 3 * i + j] for j in range(3)] for i in range(3)]
-    gain = lambda h, which: gain_ref[first_gain + 9 + PER_HOUR * h + which]
+    stay, once, both = (gain_ref[first_gain + i] for i in range(MOVES))
+    gain = lambda h, which: gain_ref[first_gain + MOVES + PER_HOUR * h + which]
     scaled = []
     mean = None
     for h in range(hours):
@@ -256,7 +252,11 @@
             error = seen
             mean = [gain(h, j) * error for j in range(3)]
         else:
-            ahead = [a[i][0] * mean[0] + a[i][1] * mean[1] + a[i][2] * mean[2] for i in range(3)]
+            ahead = [
+                stay * mean[0] + once * mean[1] + both * mean[2],
+                stay * mean[1] + once * mean[2],
+                stay * mean[2],
+            ]
             error = seen - ahead[0]
             mean = [ahead[j] + gain(h, j) * error for j in range(3)]
         scaled.append(error * gain(h, 3))
@@ -268,10 +268,14 @@
         here = slice(h * SUB, (h + 1) * SUB)
         series[here, :] = series[here, :] - gain(h, 4) * drop
         if adjoint is None:
-            adjoint = [-(a[0][j] * drop) for j in range(3)]
+            adjoint = [-(move * drop) for move in (stay, once, both)]
         else:
             less = adjoint[0] - drop
-            adjoint = [a[0][j] * less + a[1][j] * adjoint[1] + a[2][j] * adjoint[2] for j in range(3)]
+            adjoint = [
+                stay * less,
+                once * less + stay * adjoint[1],
+                both * less + once * adjoint[1] + stay * adjoint[2],
+            ]
 
     grid[...] = product(series[...], later_ref[depth : 2 * depth, :])
     turned[...] = jnp.zeros_like(turned)
@@ -350,7 +354,7 @@
         functools.partial(analyse_kernel, bands),
         out_shape=(
             jax.ShapeDtypeStruct((owners, lanes), F32),
-            jax.ShapeDtypeStruct((turns.shape[0] + 9 + PER_HOUR * hours, SUB, lat_pad), F32),
+            jax.ShapeDtypeStruct((turns.shape[0] + MOVES + PER_HOUR * hours, SUB, lat_pad), F32),
             jax.ShapeDtypeStruct(later.shape, BF16),
         ),
         in_specs=[hbm] * 7,

time: 51 us -> 50.9 us (level)
  no operation moved by 1% of the time
where the time goes in v8:
time: 50.9 us; the launch traced here: 50.7 us
  blocking collectives  46.4 us (91%)
  Pallas kernels  4.36 us (9%)
    all_to_all x1, blocking collectives, per_device(): lax.all_to_all(sent, ('tm', 'space'), split_axis=0, concat_axis=0, tiled=...  28.1 us
    all_to_all x1, blocking collectives, per_device(): lax.all_to_all(smooth, ('tm', 'space'), split_axis=0, concat_axis=0, tile...  18.2 us
    pallas_call x1, Pallas kernels, per_device(): pl.pallas_call(functools.partial(analyse_kernel, bands), out_shape=(jax.S...  2.04 us
    pallas_call x1, Pallas kernels, per_device(): pl.pallas_call(functools.partial(synthesise_kernel, bands, slots), out_sh...  1.26 us
    pallas_call x1, Pallas kernels, per_device(): pl.pallas_call(functools.partial(smooth_kernel, lat_dev, bands, turns.sha...  1.07 us

profile of v8, /device:TPU:1, one launch (start us, length us, event | category | flops | bytes accessed | tf_op | source)
XLA Modules:
  0.0 50.7 jit_solution(7599504355932251994)
XLA Ops:
  0.0 2.0 %analyse.1 = (f32[256,128]{1,0:T(8,128)S(1)}, f32[92,8,256]{2,1,0:T(8,128)S(1)}, bf16[4096,256]{1,0:T(8,128)(2,1)S(1)}) custom-call(f32[6,2,1440]{2,1,0:T(2,128)} %bitcast.14, f32[6,144,256]{2,1,0:T(8,128)} %constant.6.clone.table_hbm, f32[16]{0:T(128)} %noise_hbm.1, f32[45,192]{1,0:T(8,128)} %var_hbm.1, f32[45,192]{1,0:T(8,128)} %scale_hbm.1, ...), custom_call_target="tpu_custom_call" | custom-call | tf_op jit(solution)/shard_map/analyse/pallas_call | solution.py:353
  2.1 28.1 %all_to_all.22 = f32[256,1,128]{2,1,0:T(1,128)S(1)} all-to-all(f32[256,1,128]{2,1,0:T(1,128)S(1)} %bitcast.13), channel_id=1, replica_groups=mesh['tm'=8,'space'=32] {'tm','space'}, dimensions={0} | all-to-all | bytes 262144 | tf_op jit(solution)/shard_map/all_to_all | solution.py:378
  30.2 1.1 %smooth.1 = f32[256,128]{1,0:T(8,128)S(1)} custom-call(f32[256,128]{1,0:T(8,128)S(1)} %bitcast.11, f32[92,8,256]{2,1,0:T(8,128)S(1)} %get-tuple-element.9.gain_ref.turns_ref, bf16[4096,256]{1,0:T(8,128)(2,1)S(1)} %get-tuple-element.10.later_ref), custom_call_target="tpu_custom_call" | custom-call | tf_op jit(solution)/shard_map/smooth/pallas_call | solution.py:380
  31.2 18.2 %all_to_all.23 = f32[256,1,128]{2,1,0:T(1,128)S(1)} all-to-all(f32[256,1,128]{2,1,0:T(1,128)S(1)} %bitcast.12), channel_id=1, replica_groups=mesh['tm'=8,'space'=32] {'tm','space'}, dimensions={0} | all-to-all | bytes 262144 | tf_op jit(solution)/shard_map/all_to_all | solution.py:393
  49.5 1.3 %synthesise.1 = f32[6,2,1440]{2,1,0:T(2,128)} custom-call(f32[256,128]{1,0:T(8,128)S(1)} %bitcast.10, bf16[4096,256]{1,0:T(8,128)(2,1)S(1)} %get-tuple-element.10.later_ref, f32[92,8,256]{2,1,0:T(8,128)S(1)} %get-tuple-element.9.gain_ref.turns_ref), custom_call_target="tpu_custom_call" | custom-call | tf_op jit(solution)/shard_map/synthesise/pallas_call | solution.py:395

commit v9 on v8

--- a/solution.py
+++ b/solution.py
@@ -200,7 +200,7 @@
     fill_gains(slots, turns_hbm.shape[0], gain_ref, noise_ref, var_ref, scale_ref, var, scale)
     fetch[3].wait()
     for lat in range(lats):
-        flat[lat * hours : (lat + 1) * hours, :] = x[lat]
+        flat[lat * hours : (lat + 1) * hours, :lon] = x[lat]
     for b in range(steps):
         blocks[b * rows : (b + 1) * rows, :STEP] = flat[:, b * STEP : (b + 1) * STEP]
     value = spread(blocks[...])
@@ -325,7 +325,7 @@
     for b in range(steps):
         flat[:, b * STEP_BACK : (b + 1) * STEP_BACK] = total[b * rows : (b + 1) * rows, :STEP_BACK]
     for lat in range(lats):
-        out_ref[lat] = flat[lat * hours : (lat + 1) * hours, :]
+        out_ref[lat] = flat[lat * hours : (lat + 1) * hours, :lon]
 
 
 def params(mib):
@@ -345,6 +345,7 @@
     lat_pad = later.shape[-1]
     rows = 2 * SUB
     lanes = SUB * rows
+    lon_pad = -(-lon_size // LANES) * LANES
     vmem = pl.BlockSpec(memory_space=pltpu.VMEM)
     smem = pl.BlockSpec(memory_space=pltpu.SMEM)
     hbm = pl.BlockSpec(memory_space=pltpu.HBM)
@@ -362,7 +363,7 @@
         scratch_shapes=[
             pltpu.VMEM(by_lat.shape, F32),
             pltpu.VMEM(lon_into.shape, F32),
-            pltpu.VMEM((rows, lon_size), F32),
+            pltpu.VMEM((rows, lon_pad), F32),
             pltpu.VMEM((lon_size // STEP * rows, LANES), F32),
             pltpu.VMEM((lanes, owners), F32),
             pltpu.SMEM(noise_var.shape, F32),
@@ -397,7 +398,7 @@
         out_shape=jax.ShapeDtypeStruct(by_lat.shape, F32),
         in_specs=[vmem] * 3,
         out_specs=vmem,
-        scratch_shapes=[pltpu.VMEM((lanes, owners), F32), pltpu.VMEM((rows, lon_size), F32)],
+        scratch_shapes=[pltpu.VMEM((lanes, owners), F32), pltpu.VMEM((rows, lon_pad), F32)],
         compiler_params=params(16),
         name="synthesise",
     )(back, later, gains)

time: 50.9 us -> 50.9 us (level)
  no operation moved by 1% of the time
where the time goes in v9:
time: 50.9 us; the launch traced here: 50.7 us
  blocking collectives  46.4 us (91%)
  Pallas kernels  4.36 us (9%)
    all_to_all x1, blocking collectives, per_device(): lax.all_to_all(sent, ('tm', 'space'), split_axis=0, concat_axis=0, tiled=...  28.1 us
    all_to_all x1, blocking collectives, per_device(): lax.all_to_all(smooth, ('tm', 'space'), split_axis=0, concat_axis=0, tile...  18.2 us
    pallas_call x1, Pallas kernels, per_device(): pl.pallas_call(functools.partial(analyse_kernel, bands), out_shape=(jax.S...  2.04 us
    pallas_call x1, Pallas kernels, per_device(): pl.pallas_call(functools.partial(synthesise_kernel, bands, slots), out_sh...  1.26 us
    pallas_call x1, Pallas kernels, per_device(): pl.pallas_call(functools.partial(smooth_kernel, lat_dev, bands, turns.sha...  1.07 us

profile of v9, /device:TPU:1, one launch (start us, length us, event | category | flops | bytes accessed | tf_op | source)
XLA Modules:
  0.0 50.7 jit_solution(5985993081440150811)
XLA Ops:
  0.0 2.0 %analyse.1 = (f32[256,128]{1,0:T(8,128)S(1)}, f32[92,8,256]{2,1,0:T(8,128)S(1)}, bf16[4096,256]{1,0:T(8,128)(2,1)S(1)}) custom-call(f32[6,2,1440]{2,1,0:T(2,128)} %bitcast.14, f32[6,144,256]{2,1,0:T(8,128)} %constant.6.clone.table_hbm, f32[16]{0:T(128)} %noise_hbm.1, f32[45,192]{1,0:T(8,128)} %var_hbm.1, f32[45,192]{1,0:T(8,128)} %scale_hbm.1, ...), custom_call_target="tpu_custom_call" | custom-call | tf_op jit(solution)/shard_map/analyse/pallas_call | solution.py:354
  2.1 28.1 %all_to_all.22 = f32[256,1,128]{2,1,0:T(1,128)S(1)} all-to-all(f32[256,1,128]{2,1,0:T(1,128)S(1)} %bitcast.13), channel_id=1, replica_groups=mesh['tm'=8,'space'=32] {'tm','space'}, dimensions={0} | all-to-all | bytes 262144 | tf_op jit(solution)/shard_map/all_to_all | solution.py:379
  30.2 1.1 %smooth.1 = f32[256,128]{1,0:T(8,128)S(1)} custom-call(f32[256,128]{1,0:T(8,128)S(1)} %bitcast.11, f32[92,8,256]{2,1,0:T(8,128)S(1)} %get-tuple-element.9.gain_ref.turns_ref, bf16[4096,256]{1,0:T(8,128)(2,1)S(1)} %get-tuple-element.10.later_ref), custom_call_target="tpu_custom_call" | custom-call | tf_op jit(solution)/shard_map/smooth/pallas_call | solution.py:381
  31.2 18.2 %all_to_all.23 = f32[256,1,128]{2,1,0:T(1,128)S(1)} all-to-all(f32[256,1,128]{2,1,0:T(1,128)S(1)} %bitcast.12), channel_id=1, replica_groups=mesh['tm'=8,'space'=32] {'tm','space'}, dimensions={0} | all-to-all | bytes 262144 | tf_op jit(solution)/shard_map/all_to_all | solution.py:394
  49.5 1.3 %synthesise.1 = f32[6,2,1440]{2,1,0:T(2,128)} custom-call(f32[256,128]{1,0:T(8,128)S(1)} %bitcast.10, bf16[4096,256]{1,0:T(8,128)(2,1)S(1)} %get-tuple-element.10.later_ref, f32[92,8,256]{2,1,0:T(8,128)S(1)} %get-tuple-element.9.gain_ref.turns_ref), custom_call_target="tpu_custom_call" | custom-call | tf_op jit(solution)/shard_map/synthesise/pallas_call | solution.py:396

commit v10 on v9

--- a/solution.py
+++ b/solution.py
@@ -81,9 +81,10 @@
     by_lat = lat_basis(lat_size).reshape(lat_size, bands, lat_size // bands)
     by_lat = by_lat.transpose(0, 2, 1).reshape(lat_size, lat_size)
     pad = -lat_size % (2 * LANES)
-    by_lat = np.pad(by_lat, ((0, pad), (0, pad)))
-    later = np.concatenate([halves(by_lat.T), halves(by_lat), back], axis=0)
-    return into.astype(np.float32), later, turns.reshape(-1, SUB, owners)
+    by_lat = [np.pad(each, ((0, 0), (0, pad))) for each in (by_lat.T, by_lat)]
+    later = np.concatenate([*map(halves, by_lat), back], axis=0)
+    into = np.concatenate([into.reshape(-1, owners), turns.reshape(-1, owners)], axis=0)
+    return into.astype(np.float32), later
 
 
 def split(value):
@@ -102,13 +103,10 @@
     return both[:rows] + both[rows:] + jnp.dot(high, table_low, preferred_element_type=F32)
 
 
-def facing(table):
+def product(value, table):
     depth = table.shape[0] // 2
-    return [table[:depth], table[:depth], table[depth:]]
-
-
-def product(value, table):
-    return jnp.dot(spread(value), jnp.concatenate(facing(table), axis=0), preferred_element_type=F32)
+    high, low = split(value[:, :depth])
+    return folded_product(high, low, table[:depth], table[depth:])
 
 
 def partners(value, bands):
@@ -173,12 +171,13 @@
 
 
 def analyse_kernel(
-    bands, x_hbm, table_hbm, noise_hbm, var_hbm, scale_hbm, turns_hbm, later_hbm, out_ref, gain_ref,
+    bands, slots, x_hbm, table_hbm, noise_hbm, var_hbm, scale_hbm, later_hbm, out_ref, gain_ref,
     later_ref, x, table, flat, blocks, slots_of, noise_ref, var_ref, scale_ref, var, scale, sems,
 ):
     lats, hours, lon = x.shape
-    slots = table.shape[0]
     steps = lon // STEP
+    depth = STEP + 2 * steps
+    turns = (table.shape[0] - slots * depth) // SUB
     rows = 2 * SUB
     pairs = (
         (var_hbm, var_ref),
@@ -186,7 +185,6 @@
         (noise_hbm, noise_ref),
         (x_hbm, x),
         (table_hbm, table),
-        (turns_hbm, gain_ref.at[: turns_hbm.shape[0]]),
         (later_hbm, later_ref),
     )
     fetch = [pltpu.make_async_copy(here, there, sems.at[i]) for i, (here, there) in enumerate(pairs)]
@@ -197,7 +195,7 @@
     slots_of[...] = jnp.zeros_like(slots_of)
     for copy in fetch[:3]:
         copy.wait()
-    fill_gains(slots, turns_hbm.shape[0], gain_ref, noise_ref, var_ref, scale_ref, var, scale)
+    fill_gains(slots, turns, gain_ref, noise_ref, var_ref, scale_ref, var, scale)
     fetch[3].wait()
     for lat in range(lats):
         flat[lat * hours : (lat + 1) * hours, :lon] = x[lat]
@@ -205,14 +203,16 @@
         blocks[b * rows : (b + 1) * rows, :STEP] = flat[:, b * STEP : (b + 1) * STEP]
     value = spread(blocks[...])
     fetch[4].wait()
+    for i in range(turns):
+        gain_ref[i] = table[slots * depth + i * SUB : slots * depth + (i + 1) * SUB, :]
     for m in range(slots):
-        high, low = split(table[m, :LANES, :])
+        high, low = split(table[m * depth : m * depth + LANES, :])
         part = jnp.dot(value, jnp.concatenate([high, high, low], axis=0), preferred_element_type=F32)
         straight = crossed = None
         for b in range(steps):
             here = part[b * rows : (b + 1) * rows]
-            plain = here * table[m, STEP + b : STEP + b + 1, :]
-            cross = here * table[m, STEP + steps + b : STEP + steps + b + 1, :]
+            plain = here * table[m * depth + STEP + b : m * depth + STEP + b + 1, :]
+            cross = here * table[m * depth + STEP + steps + b : m * depth + STEP + steps + b + 1, :]
             straight = plain if straight is None else straight + plain
             crossed = cross if crossed is None else crossed + cross
         slots_of[m * rows : (m + 1) * rows, :] = straight + partners(crossed, bands)
@@ -231,8 +231,7 @@
     for part in range(parts):
         turned[part] = x_ref[part * width : (part + 1) * width, :].T
     per_part = width // bands
-    depth = 2 * grid.shape[1]
-    grid[:, lats * bands :] = jnp.zeros((grid.shape[0], grid.shape[1] - lats * bands), F32)
+    depth = 2 * lats * bands
     for h in range(per_block):
         for lat in range(lats):
             for part in range(parts):
@@ -278,7 +277,6 @@
             ]
 
     grid[...] = product(series[...], later_ref[depth : 2 * depth, :])
-    turned[...] = jnp.zeros_like(turned)
     for h in range(per_block):
         for lat in range(lats):
             for part in range(parts):
@@ -337,11 +335,13 @@
 
 
 def per_device(tables, observed, noise_var, spectral_var, time_scale):
-    lon_into, later, turns = tables
+    lon_into, later = tables
     hours_dev, lat_dev, lon_size = observed.shape
     hours = noise_var.shape[0]
     bands = lax.axis_size("space")
-    slots, _, owners = lon_into.shape
+    owners = lon_into.shape[1]
+    slots = -(-spectral_var.shape[0] // lax.axis_size("tm"))
+    turns = 2 * slots * (lon_size // STEP_BACK) // SUB
     lat_pad = later.shape[-1]
     rows = 2 * SUB
     lanes = SUB * rows
@@ -352,13 +352,13 @@
 
     by_lat = observed.transpose(1, 0, 2)
     sent, gains, later = pl.pallas_call(
-        functools.partial(analyse_kernel, bands),
+        functools.partial(analyse_kernel, bands, slots),
         out_shape=(
             jax.ShapeDtypeStruct((owners, lanes), F32),
-            jax.ShapeDtypeStruct((turns.shape[0] + MOVES + PER_HOUR * hours, SUB, lat_pad), F32),
+            jax.ShapeDtypeStruct((turns + MOVES + PER_HOUR * hours, SUB, lat_pad), F32),
             jax.ShapeDtypeStruct(later.shape, BF16),
         ),
-        in_specs=[hbm] * 7,
+        in_specs=[hbm] * 6,
         out_specs=(vmem,) * 3,
         scratch_shapes=[
             pltpu.VMEM(by_lat.shape, F32),
@@ -371,15 +371,15 @@
             pltpu.VMEM(spectral_var.shape, F32),
             pltpu.VMEM((SUB, lat_pad), F32),
             pltpu.VMEM((SUB, lat_pad), F32),
-            pltpu.SemaphoreType.DMA((7,)),
+            pltpu.SemaphoreType.DMA((6,)),
         ],
         compiler_params=params(16),
         name="analyse",
-    )(*(in_hbm(each) for each in (by_lat, lon_into, noise_var, spectral_var, time_scale, turns, later)))
+    )(*(in_hbm(each) for each in (by_lat, lon_into, noise_var, spectral_var, time_scale, later)))
     got = lax.all_to_all(sent, ("tm", "space"), split_axis=0, concat_axis=0, tiled=True)
 
     smooth = pl.pallas_call(
-        functools.partial(smooth_kernel, lat_dev, bands, turns.shape[0]),
+        functools.partial(smooth_kernel, lat_dev, bands, turns),
         out_shape=jax.ShapeDtypeStruct((owners, lanes), F32),
         in_specs=[vmem] * 3,
         out_specs=vmem,

time: 50.9 us -> 50.9 us (level)
  no operation moved by 1% of the time
where the time goes in v10:
time: 50.9 us; the launch traced here: 50.7 us
  blocking collectives  46.4 us (91%)
  Pallas kernels  4.35 us (9%)
    all_to_all x1, blocking collectives, per_device(): lax.all_to_all(sent, ('tm', 'space'), split_axis=0, concat_axis=0, tiled=...  28.1 us
    all_to_all x1, blocking collectives, per_device(): lax.all_to_all(smooth, ('tm', 'space'), split_axis=0, concat_axis=0, tile...  18.2 us
    pallas_call x1, Pallas kernels, per_device(): pl.pallas_call(functools.partial(analyse_kernel, bands, slots), out_shape...  2.02 us
    pallas_call x1, Pallas kernels, per_device(): pl.pallas_call(functools.partial(synthesise_kernel, bands, slots), out_sh...  1.26 us
    pallas_call x1, Pallas kernels, per_device(): pl.pallas_call(functools.partial(smooth_kernel, lat_dev, bands, turns), o...  1.07 us

profile of v10, /device:TPU:1, one launch (start us, length us, event | category | flops | bytes accessed | tf_op | source)
XLA Modules:
  0.0 50.7 jit_solution(9478168668275738724)
XLA Ops:
  0.0 2.0 %analyse.1 = (f32[256,128]{1,0:T(8,128)S(1)}, f32[92,8,256]{2,1,0:T(8,128)S(1)}, bf16[3840,256]{1,0:T(8,128)(2,1)S(1)}) custom-call(f32[6,2,1440]{2,1,0:T(2,128)} %bitcast.14, f32[936,256]{1,0:T(8,128)} %constant.4.clone.table_hbm, f32[16]{0:T(128)} %noise_hbm.1, f32[45,192]{1,0:T(8,128)} %var_hbm.1, f32[45,192]{1,0:T(8,128)} %scale_hbm.1, ...), custom_call_target="tpu_custom_call" | custom-call | tf_op jit(solution)/shard_map/analyse/pallas_call | solution.py:354
  2.0 28.1 %all_to_all.22 = f32[256,1,128]{2,1,0:T(1,128)S(1)} all-to-all(f32[256,1,128]{2,1,0:T(1,128)S(1)} %bitcast.13), channel_id=1, replica_groups=mesh['tm'=8,'space'=32] {'tm','space'}, dimensions={0} | all-to-all | bytes 262144 | tf_op jit(solution)/shard_map/all_to_all | solution.py:379
  30.1 1.1 %smooth.1 = f32[256,128]{1,0:T(8,128)S(1)} custom-call(f32[256,128]{1,0:T(8,128)S(1)} %bitcast.11, f32[92,8,256]{2,1,0:T(8,128)S(1)} %get-tuple-element.9.gain_ref.turns_ref, bf16[3840,256]{1,0:T(8,128)(2,1)S(1)} %get-tuple-element.10.later_ref), custom_call_target="tpu_custom_call" | custom-call | tf_op jit(solution)/shard_map/smooth/pallas_call | solution.py:381
  31.2 18.2 %all_to_all.23 = f32[256,1,128]{2,1,0:T(1,128)S(1)} all-to-all(f32[256,1,128]{2,1,0:T(1,128)S(1)} %bitcast.12), channel_id=1, replica_groups=mesh['tm'=8,'space'=32] {'tm','space'}, dimensions={0} | all-to-all | bytes 262144 | tf_op jit(solution)/shard_map/all_to_all | solution.py:394
  49.5 1.3 %synthesise.1 = f32[6,2,1440]{2,1,0:T(2,128)} custom-call(f32[256,128]{1,0:T(8,128)S(1)} %bitcast.10, bf16[3840,256]{1,0:T(8,128)(2,1)S(1)} %get-tuple-element.10.later_ref, f32[92,8,256]{2,1,0:T(8,128)S(1)} %get-tuple-element.9.gain_ref.turns_ref), custom_call_target="tpu_custom_call" | custom-call | tf_op jit(solution)/shard_map/synthesise/pallas_call | solution.py:396

commit v11 on v10

--- a/solution.py
+++ b/solution.py
@@ -251,30 +251,27 @@
             error = seen
             mean = [gain(h, j) * error for j in range(3)]
         else:
-            ahead = [
-                stay * mean[0] + once * mean[1] + both * mean[2],
-                stay * mean[1] + once * mean[2],
-                stay * mean[2],
-            ]
-            error = seen - ahead[0]
+            kept, shift = stay * mean[0], once * mean[1] + both * mean[2]
+            ahead = [kept + shift, stay * mean[1] + once * mean[2], stay * mean[2]]
+            error = (seen - kept) - shift
             mean = [ahead[j] + gain(h, j) * error for j in range(3)]
         scaled.append(error * gain(h, 3))
     adjoint = None
     for h in reversed(range(hours)):
         drop = scaled[h]
         if adjoint is not None:
-            drop = drop + (gain(h, 0) * adjoint[0] + gain(h, 1) * adjoint[1] + gain(h, 2) * adjoint[2])
+            drop = (drop + gain(h, 0) * adjoint[0]) + (gain(h, 1) * adjoint[1] + gain(h, 2) * adjoint[2])
         here = slice(h * SUB, (h + 1) * SUB)
         series[here, :] = series[here, :] - gain(h, 4) * drop
         if adjoint is None:
             adjoint = [-(move * drop) for move in (stay, once, both)]
         else:
-            less = adjoint[0] - drop
-            adjoint = [
-                stay * less,
-                once * less + stay * adjoint[1],
-                both * less + once * adjoint[1] + stay * adjoint[2],
+            moved = [
+                stay * adjoint[0],
+                once * adjoint[0] + stay * adjoint[1],
+                both * adjoint[0] + (once * adjoint[1] + stay * adjoint[2]),
             ]
+            adjoint = [value - move * drop for value, move in zip(moved, (stay, once, both))]
 
     grid[...] = product(series[...], later_ref[depth : 2 * depth, :])
     for h in range(per_block):

time: 50.9 us -> 50.8 us (level)
  no operation moved by 1% of the time
where the time goes in v11:
time: 50.8 us; the launch traced here: 50.7 us
  blocking collectives  46.4 us (91%)
  Pallas kernels  4.32 us (9%)
    all_to_all x1, blocking collectives, per_device(): lax.all_to_all(sent, ('tm', 'space'), split_axis=0, concat_axis=0, tiled=...  28.1 us
    all_to_all x1, blocking collectives, per_device(): lax.all_to_all(smooth, ('tm', 'space'), split_axis=0, concat_axis=0, tile...  18.2 us
    pallas_call x1, Pallas kernels, per_device(): pl.pallas_call(functools.partial(analyse_kernel, bands, slots), out_shape...  2.02 us
    pallas_call x1, Pallas kernels, per_device(): pl.pallas_call(functools.partial(synthesise_kernel, bands, slots), out_sh...  1.26 us
    pallas_call x1, Pallas kernels, per_device(): pl.pallas_call(functools.partial(smooth_kernel, lat_dev, bands, turns), o...  1.04 us

profile of v11, /device:TPU:1, one launch (start us, length us, event | category | flops | bytes accessed | tf_op | source)
XLA Modules:
  0.0 50.7 jit_solution(6466924504284772716)
XLA Ops:
  0.0 2.0 %analyse.1 = (f32[256,128]{1,0:T(8,128)S(1)}, f32[92,8,256]{2,1,0:T(8,128)S(1)}, bf16[3840,256]{1,0:T(8,128)(2,1)S(1)}) custom-call(f32[6,2,1440]{2,1,0:T(2,128)} %bitcast.14, f32[936,256]{1,0:T(8,128)} %constant.4.clone.table_hbm, f32[16]{0:T(128)} %noise_hbm.1, f32[45,192]{1,0:T(8,128)} %var_hbm.1, f32[45,192]{1,0:T(8,128)} %scale_hbm.1, ...), custom_call_target="tpu_custom_call" | custom-call | tf_op jit(solution)/shard_map/analyse/pallas_call | solution.py:351
  2.0 28.1 %all_to_all.22 = f32[256,1,128]{2,1,0:T(1,128)S(1)} all-to-all(f32[256,1,128]{2,1,0:T(1,128)S(1)} %bitcast.13), channel_id=1, replica_groups=mesh['tm'=8,'space'=32] {'tm','space'}, dimensions={0} | all-to-all | bytes 262144 | tf_op jit(solution)/shard_map/all_to_all | solution.py:376
  30.1 1.0 %smooth.1 = f32[256,128]{1,0:T(8,128)S(1)} custom-call(f32[256,128]{1,0:T(8,128)S(1)} %bitcast.11, f32[92,8,256]{2,1,0:T(8,128)S(1)} %get-tuple-element.9.gain_ref.turns_ref, bf16[3840,256]{1,0:T(8,128)(2,1)S(1)} %get-tuple-element.10.later_ref), custom_call_target="tpu_custom_call" | custom-call | tf_op jit(solution)/shard_map/smooth/pallas_call | solution.py:378
  31.2 18.2 %all_to_all.23 = f32[256,1,128]{2,1,0:T(1,128)S(1)} all-to-all(f32[256,1,128]{2,1,0:T(1,128)S(1)} %bitcast.12), channel_id=1, replica_groups=mesh['tm'=8,'space'=32] {'tm','space'}, dimensions={0} | all-to-all | bytes 262144 | tf_op jit(solution)/shard_map/all_to_all | solution.py:391
  49.4 1.3 %synthesise.1 = f32[6,2,1440]{2,1,0:T(2,128)} custom-call(f32[256,128]{1,0:T(8,128)S(1)} %bitcast.10, bf16[3840,256]{1,0:T(8,128)(2,1)S(1)} %get-tuple-element.10.later_ref, f32[92,8,256]{2,1,0:T(8,128)S(1)} %get-tuple-element.9.gain_ref.turns_ref), custom_call_target="tpu_custom_call" | custom-call | tf_op jit(solution)/shard_map/synthesise/pallas_call | solution.py:393

commit v12 on v11

--- a/solution.py
+++ b/solution.py
@@ -289,7 +289,7 @@
         out_ref[part * width : (part + 1) * width, :] = turned[part].T
 
 
-def synthesise_kernel(bands, slots, x_ref, later_ref, turns_ref, out_ref, turned, flat):
+def synthesise_kernel(bands, slots, x_ref, later_ref, turns_ref, out_ref, turned):
     lats, hours, lon = out_ref.shape
     steps = lon // STEP_BACK
     rows = 2 * SUB
@@ -317,10 +317,9 @@
     high = jnp.concatenate([each[0] for each in values], axis=1)
     low = jnp.concatenate([each[1] for each in values], axis=1)
     total = folded_product(high, low, jnp.concatenate(highs, axis=0), jnp.concatenate(lows, axis=0))
-    for b in range(steps):
-        flat[:, b * STEP_BACK : (b + 1) * STEP_BACK] = total[b * rows : (b + 1) * rows, :STEP_BACK]
+    field = jnp.concatenate([total[b * rows : (b + 1) * rows, :STEP_BACK] for b in range(steps)], axis=1)
     for lat in range(lats):
-        out_ref[lat] = flat[lat * hours : (lat + 1) * hours, :lon]
+        out_ref[lat] = field[lat * hours : (lat + 1) * hours, :]
 
 
 def params(mib):
@@ -395,7 +394,7 @@
         out_shape=jax.ShapeDtypeStruct(by_lat.shape, F32),
         in_specs=[vmem] * 3,
         out_specs=vmem,
-        scratch_shapes=[pltpu.VMEM((lanes, owners), F32), pltpu.VMEM((rows, lon_pad), F32)],
+        scratch_shapes=[pltpu.VMEM((lanes, owners), F32)],
         compiler_params=params(16),
         name="synthesise",
     )(back, later, gains)

time: 50.8 us -> 50.8 us (level)
  no operation moved by 1% of the time
where the time goes in v12:
time: 50.8 us; the launch traced here: 50.7 us
  blocking collectives  46.4 us (91%)
  Pallas kernels  4.3 us (8%)
    all_to_all x1, blocking collectives, per_device(): lax.all_to_all(sent, ('tm', 'space'), split_axis=0, concat_axis=0, tiled=...  28.1 us
    all_to_all x1, blocking collectives, per_device(): lax.all_to_all(smooth, ('tm', 'space'), split_axis=0, concat_axis=0, tile...  18.2 us
    pallas_call x1, Pallas kernels, per_device(): pl.pallas_call(functools.partial(analyse_kernel, bands, slots), out_shape...  2.02 us
    pallas_call x1, Pallas kernels, per_device(): pl.pallas_call(functools.partial(synthesise_kernel, bands, slots), out_sh...  1.24 us
    pallas_call x1, Pallas kernels, per_device(): pl.pallas_call(functools.partial(smooth_kernel, lat_dev, bands, turns), o...  1.04 us

profile of v12, /device:TPU:1, one launch (start us, length us, event | category | flops | bytes accessed | tf_op | source)
XLA Modules:
  0.0 50.7 jit_solution(5465975085180966467)
XLA Ops:
  0.0 2.0 %analyse.1 = (f32[256,128]{1,0:T(8,128)S(1)}, f32[92,8,256]{2,1,0:T(8,128)S(1)}, bf16[3840,256]{1,0:T(8,128)(2,1)S(1)}) custom-call(f32[6,2,1440]{2,1,0:T(2,128)} %bitcast.14, f32[936,256]{1,0:T(8,128)} %constant.4.clone.table_hbm, f32[16]{0:T(128)} %noise_hbm.1, f32[45,192]{1,0:T(8,128)} %var_hbm.1, f32[45,192]{1,0:T(8,128)} %scale_hbm.1, ...), custom_call_target="tpu_custom_call" | custom-call | tf_op jit(solution)/shard_map/analyse/pallas_call | solution.py:350
  2.0 28.1 %all_to_all.22 = f32[256,1,128]{2,1,0:T(1,128)S(1)} all-to-all(f32[256,1,128]{2,1,0:T(1,128)S(1)} %bitcast.13), channel_id=1, replica_groups=mesh['tm'=8,'space'=32] {'tm','space'}, dimensions={0} | all-to-all | bytes 262144 | tf_op jit(solution)/shard_map/all_to_all | solution.py:375
  30.1 1.0 %smooth.1 = f32[256,128]{1,0:T(8,128)S(1)} custom-call(f32[256,128]{1,0:T(8,128)S(1)} %bitcast.11, f32[92,8,256]{2,1,0:T(8,128)S(1)} %get-tuple-element.9.gain_ref.turns_ref, bf16[3840,256]{1,0:T(8,128)(2,1)S(1)} %get-tuple-element.10.later_ref), custom_call_target="tpu_custom_call" | custom-call | tf_op jit(solution)/shard_map/smooth/pallas_call | solution.py:377
  31.2 18.2 %all_to_all.23 = f32[256,1,128]{2,1,0:T(1,128)S(1)} all-to-all(f32[256,1,128]{2,1,0:T(1,128)S(1)} %bitcast.12), channel_id=1, replica_groups=mesh['tm'=8,'space'=32] {'tm','space'}, dimensions={0} | all-to-all | bytes 262144 | tf_op jit(solution)/shard_map/all_to_all | solution.py:390
  49.4 1.2 %synthesise.1 = f32[6,2,1440]{2,1,0:T(2,128)} custom-call(f32[256,128]{1,0:T(8,128)S(1)} %bitcast.10, bf16[3840,256]{1,0:T(8,128)(2,1)S(1)} %get-tuple-element.10.later_ref, f32[92,8,256]{2,1,0:T(8,128)S(1)} %get-tuple-element.9.gain_ref.turns_ref), custom_call_target="tpu_custom_call" | custom-call | tf_op jit(solution)/shard_map/synthesise/pallas_call | solution.py:392

commit v13 on v12

--- a/solution.py
+++ b/solution.py
@@ -128,22 +128,22 @@
     rate = ROOT_FIVE / scale[...]
     damping = jnp.exp(-rate)
     half_square = 0.5 * rate * rate
-    for i, move in enumerate((damping, damping * rate, damping * half_square)):
+    stay, once, both = damping, damping * rate, damping * half_square
+    for i, move in enumerate((stay, once, both)):
         out_ref[first_gain + i] = move
-    twice = damping * damping
 
     def carried(p):
-        top = [p[0, j] + rate * p[1, j] + half_square * p[2, j] for j in range(3)]
-        middle = [p[1, j] + rate * p[2, j] for j in range(3)]
-        full = {
-            (0, 0): top[0] + rate * top[1] + half_square * top[2],
-            (0, 1): top[1] + rate * top[2],
-            (0, 2): top[2],
-            (1, 1): middle[1] + rate * middle[2],
-            (1, 2): middle[2],
-            (2, 2): p[2, 2],
+        top = [stay * p[0, j] + (once * p[1, j] + both * p[2, j]) for j in range(3)]
+        middle = [stay * p[1, j] + once * p[2, j] for j in range(3)]
+        last_one = stay * p[2, 2]
+        return {
+            (0, 0): stay * top[0] + (once * top[1] + both * top[2]),
+            (0, 1): stay * top[1] + once * top[2],
+            (0, 2): stay * top[2],
+            (1, 1): stay * middle[1] + once * middle[2],
+            (1, 2): stay * middle[2],
+            (2, 2): stay * last_one,
         }
-        return {at: twice * each for at, each in full.items()}
 
     def symmetric(upper):
         return {(i, j): upper[min(i, j), max(i, j)] for i in range(3) for j in range(3)}
@@ -158,16 +158,18 @@
         if h > 0:
             moved = carried(symmetric(cov))
             pm = {entry: moved[entry] + noise_cov[entry] for entry in moved}
-        inverse = 1.0 / (pm[0, 0] + noise)
+            inverse = 1.0 / (moved[0, 0] + (noise_cov[0, 0] + noise))
+        else:
+            inverse = 1.0 / (pm[0, 0] + noise)
         k = [pm[0, j] * inverse for j in range(3)]
         for j in range(3):
             out_ref[at + j] = k[j]
         out_ref[at + 3] = inverse
         out_ref[at + 4] = jnp.full(inverse.shape, noise, F32)
-        cov = {(0, j): noise * k[j] for j in range(3)}
+        cov = {(0, j): (noise * pm[0, j]) * inverse for j in range(3)}
         for i in (1, 2):
             for j in range(i, 3):
-                cov[i, j] = pm[i, j] - k[i] * pm[0, j]
+                cov[i, j] = pm[i, j] - (pm[0, i] * pm[0, j]) * inverse
 
 
 def analyse_kernel(

time: 50.8 us -> 50.8 us (level)
  no operation moved by 1% of the time
where the time goes in v13:
time: 50.8 us; the launch traced here: 50.7 us
  blocking collectives  46.4 us (91%)
  Pallas kernels  4.31 us (8%)
    all_to_all x1, blocking collectives, per_device(): lax.all_to_all(sent, ('tm', 'space'), split_axis=0, concat_axis=0, tiled=...  28.1 us
    all_to_all x1, blocking collectives, per_device(): lax.all_to_all(smooth, ('tm', 'space'), split_axis=0, concat_axis=0, tile...  18.2 us
    pallas_call x1, Pallas kernels, per_device(): pl.pallas_call(functools.partial(analyse_kernel, bands, slots), out_shape...  2.02 us
    pallas_call x1, Pallas kernels, per_device(): pl.pallas_call(functools.partial(synthesise_kernel, bands, slots), out_sh...  1.24 us
    pallas_call x1, Pallas kernels, per_device(): pl.pallas_call(functools.partial(smooth_kernel, lat_dev, bands, turns), o...  1.04 us

profile of v13, /device:TPU:1, one launch (start us, length us, event | category | flops | bytes accessed | tf_op | source)
XLA Modules:
  0.0 50.7 jit_solution(136535183345107560)
XLA Ops:
  0.0 2.0 %analyse.1 = (f32[256,128]{1,0:T(8,128)S(1)}, f32[92,8,256]{2,1,0:T(8,128)S(1)}, bf16[3840,256]{1,0:T(8,128)(2,1)S(1)}) custom-call(f32[6,2,1440]{2,1,0:T(2,128)} %bitcast.14, f32[936,256]{1,0:T(8,128)} %constant.4.clone.table_hbm, f32[16]{0:T(128)} %noise_hbm.1, f32[45,192]{1,0:T(8,128)} %var_hbm.1, f32[45,192]{1,0:T(8,128)} %scale_hbm.1, ...), custom_call_target="tpu_custom_call" | custom-call | tf_op jit(solution)/shard_map/analyse/pallas_call | solution.py:352
  2.0 28.1 %all_to_all.22 = f32[256,1,128]{2,1,0:T(1,128)S(1)} all-to-all(f32[256,1,128]{2,1,0:T(1,128)S(1)} %bitcast.13), channel_id=1, replica_groups=mesh['tm'=8,'space'=32] {'tm','space'}, dimensions={0} | all-to-all | bytes 262144 | tf_op jit(solution)/shard_map/all_to_all | solution.py:377
  30.2 1.0 %smooth.1 = f32[256,128]{1,0:T(8,128)S(1)} custom-call(f32[256,128]{1,0:T(8,128)S(1)} %bitcast.11, f32[92,8,256]{2,1,0:T(8,128)S(1)} %get-tuple-element.9.gain_ref.turns_ref, bf16[3840,256]{1,0:T(8,128)(2,1)S(1)} %get-tuple-element.10.later_ref), custom_call_target="tpu_custom_call" | custom-call | tf_op jit(solution)/shard_map/smooth/pallas_call | solution.py:379
  31.2 18.2 %all_to_all.23 = f32[256,1,128]{2,1,0:T(1,128)S(1)} all-to-all(f32[256,1,128]{2,1,0:T(1,128)S(1)} %bitcast.12), channel_id=1, replica_groups=mesh['tm'=8,'space'=32] {'tm','space'}, dimensions={0} | all-to-all | bytes 262144 | tf_op jit(solution)/shard_map/all_to_all | solution.py:392
  49.4 1.2 %synthesise.1 = f32[6,2,1440]{2,1,0:T(2,128)} custom-call(f32[256,128]{1,0:T(8,128)S(1)} %bitcast.10, bf16[3840,256]{1,0:T(8,128)(2,1)S(1)} %get-tuple-element.10.later_ref, f32[92,8,256]{2,1,0:T(8,128)S(1)} %get-tuple-element.9.gain_ref.turns_ref), custom_call_target="tpu_custom_call" | custom-call | tf_op jit(solution)/shard_map/synthesise/pallas_call | solution.py:394
